TPU v7x, 256 devices: a whole 4x4x8 slice. The times are simulated.
256 devices in a mesh: rep: 32 (over z_hi, x, y), fsdp: 8 (over z_lo, core).
Axes of the slice: x: 4, y: 4, z: 8 (z_hi: 2, z_lo: 4; z = z_hi * 4 + z_lo), core: 2. Of those that a mesh axis runs over, the one named last changes fastest.
Arguments:
- tokens: bfloat16 [98304, 8192], P(('rep', 'fsdp')), may hold values from -6 to 6
- key_weight: bfloat16 [32, 8192, 512], P('rep', 'fsdp'), may hold values from -0.032958984 to 0.032958984
- key_grad: bfloat16 [98304, 512], P(('rep', 'fsdp')), may hold values from -0.099609375 to 0.099609375
- norm_gain: float32 [32, 8192], P('rep'), may hold values from 0.5 to 1.5
- outer_params: float32 [128, 8192], P('fsdp'), may hold values from -6 to 6
- local_params: bfloat16 [32, 128, 8192], P('rep', 'fsdp'), may hold values from -6 to 6
- momentum: float32 [128, 8192], P('fsdp'), may hold values from -6 to 6
- outer_step: int32 [1], replicated, may hold values from 0 to 7
Outputs:
- keys: bfloat16 [98304, 512], P(('rep', 'fsdp'))
- weight_grad: float32 [32, 8192, 512], P('rep', 'fsdp')
- gain_grad: float32 [32, 8192], P('rep')
- new_outer: float32 [128, 8192], P('fsdp')
- new_momentum: float32 [128, 8192], P('fsdp')
All inputs are finite; a program needn't handle non-finite values.
Results may differ from a plain program's by a relative error of at most 0.015.
Values may be sent and summed in bfloat16 or wider, within the bound.
A program may use at most 128 MiB of HBM per device.

v0:
```python
import jax
import jax.numpy as jnp
from jax import lax
from jax.sharding import PartitionSpec as P

WARM = 8


epsilon = 1e-05
OUTER_LR = 0.7
OUTER_MOMENTUM = 0.9


def nesterov(outer_part, moment_part, pseudo, outer_rate):
    moment_next = OUTER_MOMENTUM * moment_part + pseudo
    outer_next = outer_part - outer_rate * (pseudo + OUTER_MOMENTUM * moment_next)
    return (outer_next, moment_next)


def local(
    tokens, key_weight, key_grad, norm_gain, outer_params, local_params, momentum, outer_step
):
    wide = tokens.astype(jnp.float32)
    inv_rms = lax.rsqrt(jnp.mean(wide * wide, axis=1, keepdims=True) + epsilon)
    shard = key_weight[0]
    contract_last = (((1,), (1,)), ((), ()))
    normed = (wide * inv_rms * norm_gain[0][None, :]).astype(jnp.bfloat16)
    columns = normed
    keys_wide = jnp.dot(
        columns,
        lax.all_gather(shard, "fsdp", axis=0, tiled=True),
        preferred_element_type=jnp.float32,
    )
    d_normed = lax.dot_general(
        key_grad,
        lax.all_gather(shard, "fsdp", axis=0, tiled=True),
        contract_last,
        preferred_element_type=jnp.float32,
    )
    gain_grad = lax.psum(jnp.sum(d_normed * wide * inv_rms, axis=0), "fsdp")
    columns = normed
    term = lax.dot_general(
        columns, key_grad, (((0,), (0,)), ((), ())), preferred_element_type=jnp.float32
    )
    term = lax.optimization_barrier(term.astype(jnp.bfloat16))
    weight_grad = lax.psum_scatter(
        term.astype(jnp.float32).astype(jnp.bfloat16), "fsdp", scatter_dimension=0, tiled=True
    ).astype(jnp.float32)
    keys_out = keys_wide.astype(jnp.bfloat16)
    pseudo_grad = outer_params - local_params[0].astype(jnp.float32)
    replicas = lax.axis_size("rep")
    outer_rate = OUTER_LR * (outer_step[0].astype(jnp.float32) + 1.0) / WARM
    averaged = lax.psum(pseudo_grad, "rep") / replicas
    new_outer, new_momentum = nesterov(outer_params, momentum, averaged, outer_rate)
    return (keys_out, weight_grad[None], gain_grad[None], new_outer, new_momentum)


def solution(mesh):
    placed = (
        P(("rep", "fsdp"), None),
        P("rep", "fsdp", None),
        P(("rep", "fsdp"), None),
        P("rep", None),
        P("fsdp", None),
        P("rep", "fsdp", None),
        P("fsdp", None),
        P(),
    )
    return jax.shard_map(
        local,
        mesh=mesh,
        in_specs=placed,
        out_specs=(
            P(("rep", "fsdp"), None),
            P("rep", "fsdp", None),
            P("rep", None),
            P("fsdp", None),
            P("fsdp", None),
        ),
        check_vma=False,
    )
```

profile of v0, /device:TPU:1, one launch (start us, length us, event | category | flops | bytes accessed | tf_op | source)
XLA Modules:
  0.0 588.5 jit_solution(13334433917490704919)
XLA Ops:
  8.0 0.0 copy-start
  8.0 0.0 copy-start.3
  8.0 0.0 all-reduce.2.cloned.1.call-start
  8.1 2.0 convert_subtract_fusion
  10.1 0.0 all-reduce.2.cloned.1.call-update
  10.1 0.0 all-gather.3.cloned.1.call-start
  10.1 0.5 all-gather.3.cloned.1.call-update
  10.7 0.0 reduce-scatter.2.cloned.1.call-start
  10.7 4.1 fusion
  14.8 0.0 copy-done
  14.8 0.0 copy-done.3
  14.8 10.7 %convolution_convert_fusion = bf16[8192,512]{1,0:T(8,128)(2,1)} fusion(bf16[384,512]{1,0:T(8,128)(2,1)S(1)} %copy-done, bf16[384,8192]{1,0:T(8,128)(2,1)} %param.8, f32[8192]{0:T(1024)S(1)} %bitcast.19, f32[384]{0:T(512)S(1)} %add_rsqrt_fusion), kind=kOutput, calls=%fused_computation.8 | convolution fusion | flops 3238002688 | bytes 15107584 | tf_op jit(solution)/shard_map/dot_general | solution.py:42
  25.5 0.0 copy-start.1
  25.5 0.0 copy-start.2
  25.5 0.0 reduce-scatter.2.cloned.1.call-update
  26.3 486.2 %all-reduce.2.cloned.1.call-done = f32[16,8192]{1,0:T(8,128)} async-done(((f32[16,8192]{1,0:T(8,128)}), f32[16,8192]{1,0:T(8,128)}) %all-reduce.2.cloned.1.call-update) | async-done | bytes 524304 | tf_op jit(solution)/shard_map/psum | solution.py:53
  512.4 0.0 copy-done.1
  512.4 0.0 copy-done.2
  512.4 2.1 multiply_subtract_fusion
  514.6 0.0 all-gather.3.cloned.1.call-done
  514.6 10.2 %fusion.4 = f32[8192]{0:T(1024)S(1)} fusion(bf16[384,8192]{1,0:T(8,128)(2,1)} %param.8, bf16[384,512]{1,0:T(8,128)(2,1)S(1)} %copy-done, bf16[1,8192,512]{2,1,0:T(8,128)(2,1)} %all-gather.3.cloned.1.call-done, f32[384]{0:T(512)S(1)} %add_rsqrt_fusion), kind=kOutput, calls=%fused_computation.7 | convolution fusion | flops 3233800192 | bytes 15107584 | tf_op jit(solution)/shard_map/dot_general | solution.py:34
  524.7 44.1 %psum.14 = f32[1,8192]{1,0:T(1,128)} all-reduce(f32[1,8192]{1,0:T(1,128)S(1)} %bitcast.18), channel_id=1, replica_groups=mesh['rep'=32,'fsdp'=8] {'fsdp'}, use_global_device_ids=true, to_apply=%region_3.0 | all-reduce | flops 8192 | bytes 65536 | tf_op jit(solution)/shard_map/psum | solution.py:40
  568.8 9.4 %fusion.10 = bf16[384,512]{1,0:T(8,128)(2,1)} fusion(bf16[1,8192,512]{2,1,0:T(8,128)(2,1)} %all-gather.3.cloned.1.call-done, bf16[384,8192]{1,0:T(8,128)(2,1)} %param.8, f32[8192]{0:T(1024)S(1)} %bitcast.20, f32[384]{0:T(512)S(1)} %add_rsqrt_fusion), kind=kOutput, calls=%fused_computation.12 | convolution fusion | flops 3234004992 | bytes 15107584 | tf_op jit(solution)/shard_map/dot_general | solution.py:29
  578.2 0.0 reduce-scatter.2.cloned.1.call-done
  578.2 2.8 bitcast_convert_fusion
  (1 shorter events, 0.0 us)
Async XLA Ops:
  8.0 6.8 %copy-start = (bf16[384,512]{1,0:T(8,128)(2,1)S(1)}, bf16[384,512]{1,0:T(8,128)(2,1)}, u32[]{:S(2)}) copy-start(bf16[384,512]{1,0:T(8,128)(2,1)} %param.10) | copy-start | bytes 1179652
  8.0 6.8 %copy-start.3 = (f32[1,8192]{1,0:T(1,128)S(1)}, f32[1,8192]{1,0:T(1,128)}, u32[]{:S(2)}) copy-start(f32[1,8192]{1,0:T(1,128)} %param.11) | copy-start | bytes 98308
  8.0 504.4 %all-reduce.2.cloned.1.call-start = ((), (), s32[]{:S(2)}) async-start(), calls=%async_computation.2 | async-start | bytes 1048576 | tf_op jit(solution)/shard_map/psum | solution.py:53
  10.1 504.5 %all-gather.3.cloned.1.call-start = ((), (), s32[]{:S(2)}) async-start(), calls=%async_computation.3 | async-start | bytes 9437184 | tf_op jit(solution)/shard_map/all_gather | solution.py:31
  10.7 567.6 %reduce-scatter.2.cloned.1.call-start = ((), (), s32[]{:S(2)}) async-start(), calls=%async_computation.1 | async-start | bytes 9437184 | tf_op jit(solution)/shard_map/reduce_scatter | solution.py:46
  25.5 486.9 %copy-start.1 = (f32[16,8192]{1,0:T(8,128)S(1)}, f32[16,8192]{1,0:T(8,128)}, u32[]{:S(2)}) copy-start(f32[16,8192]{1,0:T(8,128)} %param.12) | copy-start | bytes 1572868
  25.5 486.9 %copy-start.2 = (f32[16,8192]{1,0:T(8,128)S(1)}, f32[16,8192]{1,0:T(8,128)}, u32[]{:S(2)}) copy-start(f32[16,8192]{1,0:T(8,128)} %param.14) | copy-start | bytes 1572868
Sparse Core Ops, SparseCore 0:
  12.0 500.3 all-reduce.1
Sparse Core Ops, SparseCore 1:
  12.3 97.9 all-gather.2
  112.7 95.9 reduce-scatter.1
where the time goes:
time: 591 us; the launch traced here: 589 us
  waiting for transfers between devices  487 us (82%)
  blocking collectives  44.1 us (7%)
  matrix products  30.2 us (5%)
  between operations  16.3 us (3%)
  other arithmetic  11.1 us (2%)
    psum x1, waiting for transfers between devices, local(): averaged = lax.psum(pseudo_grad, 'rep') / replicas  486 us
    psum x1, blocking collectives, local(): gain_grad = lax.psum(jnp.sum(d_normed * wide * inv_rms, axis=0), 'fsdp')  44.1 us
  transfers between devices with their start and end apart: 3, of which 1 were waited for; matrix products, arithmetic and copies ran while one was open for 6% of the time, Pallas kernels for 0%

commit v1 on v0

v1 whole, which is shorter than its diff:
```python
import functools

import jax
import jax.numpy as jnp
from jax import lax
from jax.experimental import pallas as pl
from jax.experimental.pallas import tpu as pltpu
from jax.sharding import PartitionSpec as P

MESH = pl.DeviceIdType.MESH
BF16, F32 = jnp.bfloat16, jnp.float32

WARM = 8
EPSILON = 1e-05
OUTER_LR = 0.7
OUTER_MOMENTUM = 0.9

CHIPS, CORES = 4, 2
XS, YS, ZS = 4, 4, 2
CHUNKS = 4
STEPS = CHIPS * CHUNKS
AHEAD = 3
LOADS = 6
ROWS = 16
MIB = 1024 * 1024

W0, P0, S0, R0, L0 = 0, 8, 16, 20, 24
SLOTS = 28


def kernel(
    tok_hbm, kw_hbm, kg_hbm, gain_hbm, op_hbm, lp_hbm, mo_hbm, step_ref,
    keys_hbm, wg_hbm, gg_hbm, no_hbm, nm_hbm,
    tok, nrm, kg, gain, inv, buf, kacc, kout, wg,
    g_own, g_sib, g_z, g_fin,
    xr, ysum, yr, zs, zr, ps, op, mo,
    tok_sem, ld_sem, out_sem,
    r_send, r_recv, l_send, l_recv,
    w_send, w_recv, p_send, p_recv,
    g_send, g_recv, o_send, o_recv,
):
    tokens, width = tok.shape
    shard, kw = buf.shape[1:]
    part = shard // CHUNKS
    frag = op.shape[0]
    xcols, ycols = width // XS, width // XS // YS

    rep, fsdp = lax.axis_index("rep"), lax.axis_index("fsdp")
    q, x, y = rep // (XS * YS), (rep // YS) % XS, rep % YS
    z, c = fsdp // CORES, fsdp % CORES
    o = 1 - c

    def at_rep(q_, x_, y_):
        return ((q_ * XS + x_) * YS + y_, fsdp)

    def at_chip(z_):
        return (rep, z_ * CORES + c)

    sibling = (rep, z * CORES + o)
    right, left = at_chip(lax.rem(z + 1, CHIPS)), at_chip(lax.rem(z + CHIPS - 1, CHIPS))
    has_right, has_left = z < CHIPS - 1, z > 0

    def remote(src, dst, send, recv, device):
        return pltpu.make_async_remote_copy(
            src_ref=src, dst_ref=dst, send_sem=send, recv_sem=recv, device_id=device, device_id_type=MESH
        )

    def rows_of(i):
        return pl.ds(pl.multiple_of(i * part, part), part)

    block = tokens // LOADS

    def tok_load(b):
        rows = pl.ds(pl.multiple_of(b * block, block), block)
        return pltpu.make_async_copy(tok_hbm.at[rows], tok.at[rows], tok_sem.at[b])

    load_gain = pltpu.make_async_copy(gain_hbm, gain, ld_sem.at[0])
    load_kg = pltpu.make_async_copy(kg_hbm, kg, ld_sem.at[1])
    load_w = pltpu.make_async_copy(kw_hbm, buf.at[W0 + 2 * z + c], ld_sem.at[2])
    own_x = pl.ds(pl.multiple_of(x * xcols, xcols), xcols)
    load_lp = pltpu.make_async_copy(lp_hbm.at[:, own_x], xr.at[x], ld_sem.at[3])
    load_op = pltpu.make_async_copy(op_hbm, op, ld_sem.at[4])
    load_mo = pltpu.make_async_copy(mo_hbm, mo, ld_sem.at[5])

    load_gain.start()
    tok_load(0).start()
    load_kg.start()
    for b in range(1, LOADS):
        tok_load(b).start()
    for load in (load_w, load_lp, load_op, load_mo):
        load.start()

    barrier = pltpu.get_barrier_semaphore()
    peers = [at_chip(lax.rem(z + d, CHIPS)) for d in range(1, CHIPS)] + [sibling]
    peers += [at_rep(q, lax.rem(x + d, XS), y) for d in range(1, XS)]
    peers += [at_rep(q, x, lax.rem(y + d, YS)) for d in range(1, YS)]
    peers += [at_rep(1 - q, x, y)]
    for peer in peers:
        pl.semaphore_signal(barrier, inc=1, device_id=peer, device_id_type=MESH)
    pl.semaphore_wait(barrier, len(peers))

    def line_first(n, rightward):
        rows = rows_of(n)
        dst = buf.at[W0 + 2 * z + c, rows]
        if rightward:
            return remote(kw_hbm.at[rows], dst, r_send.at[n], r_recv.at[n], right)
        return remote(kw_hbm.at[rows], dst, l_send.at[n], l_recv.at[n], left)

    def line_copy(n, rightward):
        k, rows = n // CHUNKS, rows_of(n % CHUNKS)
        if rightward:
            is_sum = (k - z + CHIPS - 1) // CHIPS
            weight, owner = 2 * (z - k) + c, CHIPS + z - k
            src = (1 - is_sum) * (W0 + weight) + is_sum * (P0 + 2 * owner + c)
            dst = (1 - is_sum) * (W0 + weight) + is_sum * (R0 + owner)
            return remote(buf.at[src, rows], buf.at[dst, rows], r_send.at[n], r_recv.at[n], right)
        is_sum = (k + z) // CHIPS
        weight, owner = 2 * (z + k) + c, k + z - CHIPS
        src = (1 - is_sum) * (W0 + weight) + is_sum * (P0 + 2 * owner + c)
        dst = (1 - is_sum) * (W0 + weight) + is_sum * (L0 + owner)
        return remote(buf.at[src, rows], buf.at[dst, rows], l_send.at[n], l_recv.at[n], left)

    for n in range(CHUNKS):

        @pl.when(has_right)
        def _():
            line_first(n, True).start()

        @pl.when(has_left)
        def _():
            line_first(n, False).start()

    def own_to_sibling(i):
        rows = rows_of(i)
        return remote(
            kw_hbm.at[rows], buf.at[W0 + 2 * z + c, rows], w_send.at[z, i], w_recv.at[z, i], sibling
        )

    def to_sibling(a, i):
        there = buf.at[W0 + 2 * a + c, rows_of(i)]
        return remote(there, there, w_send.at[a, i], w_recv.at[a, i], sibling)

    def from_sibling(a, i):
        there = buf.at[W0 + 2 * a + o, rows_of(i)]
        return remote(there, there, w_send.at[a, i], w_recv.at[a, i], sibling)

    def terms_to_sibling(j, i):
        return remote(
            buf.at[P0 + 2 * j + o, rows_of(i)], buf.at[S0 + j, rows_of(i)], p_send.at[j, i], p_recv.at[j, i], sibling
        )

    for i in range(CHUNKS):
        own_to_sibling(i).start()

    def x_copy(d):
        to = lax.rem(x + d, XS)
        cols = pl.ds(pl.multiple_of(to * xcols, xcols), xcols)
        return remote(lp_hbm.at[:, cols], xr.at[x], o_send.at[0, d - 1], o_recv.at[0, d - 1], at_rep(q, to, y))

    def x_wait(d):
        slot = xr.at[lax.rem(x + XS - d, XS)]
        return remote(slot, slot, o_send.at[0, d - 1], o_recv.at[0, d - 1], sibling)

    def y_copy(d):
        to = lax.rem(y + d, YS)
        return remote(ysum.at[to], yr.at[y], o_send.at[1, d - 1], o_recv.at[1, d - 1], at_rep(q, x, to))

    def y_wait(d):
        slot = yr.at[lax.rem(y + YS - d, YS)]
        return remote(slot, slot, o_send.at[1, d - 1], o_recv.at[1, d - 1], sibling)

    z_copy = remote(zs, zr, o_send.at[2, 0], o_recv.at[2, 0], at_rep(1 - q, x, y))

    def y_back(d):
        piece = ps.at[x, y]
        return remote(
            piece, piece, o_send.at[3, d - 1], o_recv.at[3, d - 1], at_rep(q, x, lax.rem(y + d, YS))
        )

    def y_back_wait(d):
        piece = ps.at[x, lax.rem(y + YS - d, YS)]
        return remote(piece, piece, o_send.at[3, d - 1], o_recv.at[3, d - 1], sibling)

    def x_back(d):
        piece = ps.at[x]
        return remote(
            piece, piece, o_send.at[4, d - 1], o_recv.at[4, d - 1], at_rep(q, lax.rem(x + d, XS), y)
        )

    def x_back_wait(d):
        piece = ps.at[lax.rem(x + XS - d, XS)]
        return remote(piece, piece, o_send.at[4, d - 1], o_recv.at[4, d - 1], sibling)

    for d in range(1, XS):
        x_copy(d).start()

    load_gain.wait()
    lanes = 128
    pieces = width // lanes

    @pl.loop(0, LOADS)
    def _(b):
        tok_load(b).wait()

        @pl.loop(0, block // ROWS)
        def _(r):
            rows = pl.ds(pl.multiple_of(b * block + r * ROWS, ROWS), ROWS)
            sums = [jnp.zeros((ROWS, lanes), F32) for _ in range(4)]
            for m in range(pieces):
                wide = tok[rows, m * lanes : (m + 1) * lanes].astype(F32)
                sums[m % 4] = sums[m % 4] + wide * wide
            total = jnp.sum((sums[0] + sums[1]) + (sums[2] + sums[3]), axis=1, keepdims=True)
            scale = jnp.broadcast_to(lax.rsqrt(total * (1.0 / width) + EPSILON), (ROWS, lanes))
            inv[rows, :] = scale
            for m in range(pieces):
                cols = slice(m * lanes, (m + 1) * lanes)
                nrm[rows, cols] = (tok[rows, cols].astype(F32) * scale * gain[:, cols]).astype(BF16)

    load_kg.wait()
    upper = z // (CHIPS // 2)

    def cols_of(owner, i):
        return pl.ds(pl.multiple_of(owner * shard + i * part, part), part)

    def terms(owner, i):
        got = lax.dot_general(
            nrm[:, cols_of(owner, i)], kg[...], (((0,), (0,)), ((), ())), preferred_element_type=F32
        )
        buf[P0 + owner, rows_of(i), :] = got.astype(BF16)

    @pl.loop(0, STEPS)
    def _(t):
        n, i = t // CHUNKS, t % CHUNKS
        j = (1 - upper) * (CHIPS - 1 - n) + upper * n
        terms(2 * j + o, i)
        terms_to_sibling(j, i).start()
        terms(2 * j + c, i)

    kacc[...] = jnp.zeros_like(kacc)
    load_w.wait()

    def use_rows(a, core, i):
        owner = 2 * a + core
        rows = buf[W0 + owner, rows_of(i), :]
        cols = cols_of(owner, i)
        kacc[...] += jnp.dot(nrm[:, cols], rows, preferred_element_type=F32)
        d_normed = lax.dot_general(kg[...], rows, (((1,), (1,)), ((), ())), preferred_element_type=F32)
        wide = tok[:, cols].astype(F32)
        for m in range(part // lanes):
            here = slice(m * lanes, (m + 1) * lanes)
            got = jnp.sum(d_normed[:, here] * wide[:, here] * inv[...], axis=0, keepdims=True)
            g_own[core, a, pl.ds(i * (part // lanes) + m, 1), :] = got

    def use_both(a, i):
        use_rows(a, c, i)
        from_sibling(a, i).wait_recv()
        use_rows(a, o, i)

    def add_terms(j, i, base, from_line):
        rows = rows_of(i)
        terms_to_sibling(j, i).wait_recv()
        own = buf[P0 + 2 * j + c, rows, :].astype(F32) + buf[S0 + j, rows, :].astype(F32)

        @pl.when(from_line)
        def _():
            buf[P0 + 2 * j + c, rows, :] = (own + buf[base + j, rows, :].astype(F32)).astype(BF16)

        @pl.when(jnp.logical_not(from_line))
        def _():
            buf[P0 + 2 * j + c, rows, :] = own.astype(BF16)

    def write_rows(i):
        rows = rows_of(i)
        return pltpu.make_async_copy(wg.at[rows], wg_hbm.at[rows], out_sem.at[i])

    write_keys = pltpu.make_async_copy(kout, keys_hbm, out_sem.at[CHUNKS])
    write_gain = pltpu.make_async_copy(g_fin, gg_hbm, out_sem.at[CHUNKS + 1])
    write_op = pltpu.make_async_copy(op, no_hbm, out_sem.at[CHUNKS + 2])
    write_mo = pltpu.make_async_copy(mo, nm_hbm, out_sem.at[CHUNKS + 3])

    gain_swap = remote(g_own.at[o], g_sib, g_send.at[0], g_recv.at[0], sibling)

    def gain_copy(d):
        return remote(g_z.at[z], g_z.at[z], g_send.at[d], g_recv.at[d], at_chip(lax.rem(z + d, CHIPS)))

    def gain_wait(d):
        slot = g_z.at[lax.rem(z + CHIPS - d, CHIPS)]
        return remote(slot, slot, g_send.at[d], g_recv.at[d], sibling)

    gain_back = remote(g_fin.at[:, c], g_fin.at[:, c], g_send.at[CHIPS], g_recv.at[CHIPS], sibling)

    @pl.loop(0, STEPS)
    def _(s):
        k, i = s // CHUNKS, s % CHUNKS

        @pl.when(s == 2)
        def _():
            load_lp.wait()
            for d in range(1, XS):
                x_wait(d).wait_recv()
            for m in range(YS):
                cols = slice(m * ycols, (m + 1) * ycols)
                ysum[m] = (xr[0, :, cols].astype(F32) + xr[1, :, cols].astype(F32)) + (
                    xr[2, :, cols].astype(F32) + xr[3, :, cols].astype(F32)
                )
            for d in range(1, YS):
                y_copy(d).start()
            yr[y] = ysum[y]

        @pl.when(s == 3)
        def _():
            for d in range(1, YS):
                y_wait(d).wait_recv()
            load_op.wait()
            cols = pl.ds(pl.multiple_of(x * xcols + y * ycols, ycols), ycols)
            total = (yr[0] + yr[1]) + (yr[2] + yr[3])
            zs[...] = (float(XS * YS) * op[:, cols] - total).astype(BF16)
            z_copy.start()

        @pl.when(s == 8)
        def _():
            z_copy.wait_recv()
            ps[x, y] = (zs[...].astype(F32) + zr[...].astype(F32)) * (1.0 / (XS * YS * ZS))
            for d in range(1, YS):
                y_back(d).start()

        @pl.when(s == 9)
        def _():
            for d in range(1, YS):
                y_back_wait(d).wait_recv()
            for d in range(1, XS):
                x_back(d).start()

        @pl.when(s == 10)
        def _():
            for d in range(1, XS):
                x_back_wait(d).wait_recv()
            load_mo.wait()
            rate = OUTER_LR * (step_ref[0].astype(F32) + 1.0) / WARM
            for a in range(XS):
                for b in range(YS):
                    cols = slice((a * YS + b) * ycols, (a * YS + b + 1) * ycols)
                    pseudo = ps[a, b]
                    moment = OUTER_MOMENTUM * mo[:, cols] + pseudo
                    mo[:, cols] = moment
                    op[:, cols] = op[:, cols] - rate * (pseudo + OUTER_MOMENTUM * moment)
            write_op.start()
            write_mo.start()

        @pl.when(s == STEPS - 1)
        def _():
            for d in range(1, CHIPS):
                gain_wait(d).wait_recv()
            g_fin[:, c] = (g_z[0] + g_z[1]) + (g_z[2] + g_z[3])
            gain_back.start()

        @pl.when(has_left)
        def _():
            line_copy(s, True).wait_recv()

        @pl.when(has_right)
        def _():
            line_copy(s, False).wait_recv()

        left_weights = jnp.logical_and(has_left, k <= z - 1)
        right_weights = jnp.logical_and(has_right, k <= CHIPS - 2 - z)

        @pl.when(left_weights)
        def _():
            to_sibling(z - 1 - k, i).start()

        @pl.when(right_weights)
        def _():
            to_sibling(z + 1 + k, i).start()

        later = k + 1

        @pl.when(jnp.logical_and(has_right, jnp.logical_and(later < CHIPS, later > z)))
        def _():
            add_terms(CHIPS + z - later, i, R0, has_left)

        @pl.when(jnp.logical_and(has_left, jnp.logical_and(later < CHIPS, later > CHIPS - 1 - z)))
        def _():
            add_terms(later + z - CHIPS, i, L0, has_right)

        n = s + AHEAD

        @pl.when(jnp.logical_and(has_right, jnp.logical_and(n >= CHUNKS, n < STEPS)))
        def _():
            line_copy(n, True).start()

        @pl.when(jnp.logical_and(has_left, jnp.logical_and(n >= CHUNKS, n < STEPS)))
        def _():
            line_copy(n, False).start()

        @pl.when(k == CHIPS - 1)
        def _():
            rows = rows_of(i)
            terms_to_sibling(z, i).wait_recv()
            wg[rows, :] = buf[P0 + 2 * z + c, rows, :].astype(F32) + buf[S0 + z, rows, :].astype(F32)

            @pl.when(has_left)
            def _():
                wg[rows, :] += buf[R0 + z, rows, :].astype(F32)

            @pl.when(has_right)
            def _():
                wg[rows, :] += buf[L0 + z, rows, :].astype(F32)

            write_rows(i).start()

        before = s - 1 + CHUNKS
        k_before, i_before = before // CHUNKS - 1, before % CHUNKS

        @pl.when(jnp.logical_and(s > 0, jnp.logical_and(has_left, k_before <= z - 1)))
        def _():
            use_both(z - 1 - k_before, i_before)

        @pl.when(jnp.logical_and(s > 0, jnp.logical_and(has_right, k_before <= CHIPS - 2 - z)))
        def _():
            use_both(z + 1 + k_before, i_before)

        @pl.when(k == 1)
        def _():
            use_both(z, i)

        @pl.when(s == STEPS - CHUNKS)
        def _():
            gain_swap.start()
            gain_swap.wait_recv()
            g_z[z] = g_own[c] + g_sib[...]
            for d in range(1, CHIPS):
                gain_copy(d).start()
            kout[...] = kacc[...].astype(BF16)
            write_keys.start()

    gain_back_in = remote(g_fin.at[:, o], g_fin.at[:, o], g_send.at[CHIPS], g_recv.at[CHIPS], sibling)
    gain_back_in.wait_recv()
    write_gain.start()

    @pl.when(has_right)
    def _():
        @pl.loop(0, STEPS)
        def _(n):
            line_copy(n, True).wait_send()

    @pl.when(has_left)
    def _():
        @pl.loop(0, STEPS)
        def _(n):
            line_copy(n, False).wait_send()

    @pl.loop(0, STEPS)
    def _(t):
        to_sibling(t // CHUNKS, t % CHUNKS).wait_send()
        terms_to_sibling(t // CHUNKS, t % CHUNKS).wait_send()

    gain_swap.wait_send()
    gain_back.wait_send()
    for d in range(1, CHIPS):
        gain_copy(d).wait_send()
    for d in range(1, XS):
        x_copy(d).wait_send()
        x_back(d).wait_send()
    for d in range(1, YS):
        y_copy(d).wait_send()
        y_back(d).wait_send()
    z_copy.wait_send()

    for i in range(CHUNKS):
        write_rows(i).wait()
    for write in (write_keys, write_gain, write_op, write_mo):
        write.wait()


def local(tokens, key_weight, key_grad, norm_gain, outer_params, local_params, momentum, outer_step):
    rows, width = tokens.shape
    _, shard, kw = key_weight.shape
    frag = outer_params.shape[0]
    xcols, ycols = width // XS, width // XS // YS
    lanes = 128
    dma, anywhere = pltpu.SemaphoreType.DMA, pl.BlockSpec(memory_space=pl.ANY)
    keys, weight_grad, gain_grad, new_outer, new_momentum = pl.pallas_call(
        kernel,
        out_shape=(
            jax.ShapeDtypeStruct((rows, kw), BF16),
            jax.ShapeDtypeStruct((shard, kw), F32),
            jax.ShapeDtypeStruct((CHIPS, CORES, shard // lanes, lanes), F32),
            jax.ShapeDtypeStruct(outer_params.shape, F32),
            jax.ShapeDtypeStruct(momentum.shape, F32),
        ),
        in_specs=[anywhere] * 7 + [pl.BlockSpec(memory_space=pltpu.SMEM)],
        out_specs=(anywhere,) * 5,
        scratch_shapes=[
            pltpu.VMEM((rows, width), BF16),
            pltpu.VMEM((rows, width), BF16),
            pltpu.VMEM((rows, kw), BF16),
            pltpu.VMEM((1, width), F32),
            pltpu.VMEM((rows, lanes), F32),
            pltpu.VMEM((SLOTS, shard, kw), BF16),
            pltpu.VMEM((rows, kw), F32),
            pltpu.VMEM((rows, kw), BF16),
            pltpu.VMEM((shard, kw), F32),
            pltpu.VMEM((CORES, CHIPS, shard // lanes, lanes), F32),
            pltpu.VMEM((CHIPS, shard // lanes, lanes), F32),
            pltpu.VMEM((CHIPS, CHIPS, shard // lanes, lanes), F32),
            pltpu.VMEM((CHIPS, CORES, shard // lanes, lanes), F32),
            pltpu.VMEM((XS, frag, xcols), BF16),
            pltpu.VMEM((YS, frag, ycols), F32),
            pltpu.VMEM((YS, frag, ycols), F32),
            pltpu.VMEM((frag, ycols), BF16),
            pltpu.VMEM((frag, ycols), BF16),
            pltpu.VMEM((XS, YS, frag, ycols), F32),
            pltpu.VMEM((frag, width), F32),
            pltpu.VMEM((frag, width), F32),
            dma((LOADS,)),
            dma((6,)),
            dma((CHUNKS + 4,)),
            dma((STEPS,)),
            dma((STEPS,)),
            dma((STEPS,)),
            dma((STEPS,)),
            dma((CHIPS, CHUNKS)),
            dma((CHIPS, CHUNKS)),
            dma((CHIPS, CHUNKS)),
            dma((CHIPS, CHUNKS)),
            dma((CHIPS + 1,)),
            dma((CHIPS + 1,)),
            dma((5, 3)),
            dma((5, 3)),
        ],
        compiler_params=pltpu.CompilerParams(
            collective_id=0, has_side_effects=True, vmem_limit_bytes=60 * MIB
        ),
        cost_estimate=pl.CostEstimate(
            flops=6 * rows * width * kw, bytes_accessed=16 * MIB, transcendentals=rows
        ),
        name="outer_and_keys",
    )(
        tokens, key_weight[0], key_grad, norm_gain, outer_params, local_params[0], momentum, outer_step
    )
    return keys, weight_grad[None], gain_grad.reshape(1, width), new_outer, new_momentum


def solution(mesh):
    placed = (
        P(("rep", "fsdp"), None),
        P("rep", "fsdp", None),
        P(("rep", "fsdp"), None),
        P("rep", None),
        P("fsdp", None),
        P("rep", "fsdp", None),
        P("fsdp", None),
        P(),
    )
    return jax.shard_map(
        local,
        mesh=mesh,
        in_specs=placed,
        out_specs=(
            P(("rep", "fsdp"), None),
            P("rep", "fsdp", None),
            P("rep", None),
            P("fsdp", None),
            P("fsdp", None),
        ),
        check_vma=False,
    )
```

time: 591 us -> 114 us (0.19)
  waiting for transfers between devices: 487 us -> 0 us
  Pallas kernels: 0 us -> 106 us
  blocking collectives: 44.1 us -> 0 us
  matrix products: 30.2 us -> 0 us
  between operations: 16.3 us -> 1.29 us
  other arithmetic: 11.1 us -> 0 us
  local copies, waits for them, and re-layouts: 0.02 us -> 7.15 us
    psum x1 -> x0, waiting for transfers between devices: 486 us -> none  [local(): averaged = lax.psum(pseudo_grad, 'rep') / replicas]
    pallas_call x0 -> x1, Pallas kernels: none -> 106 us  [local(): pl.pallas_call(kernel, out_shape=(jax.ShapeDtypeStruct((rows, kw), BF16),...]
    psum x1 -> x0, blocking collectives: 44.1 us -> none  [local(): gain_grad = lax.psum(jnp.sum(d_normed * wide * inv_rms, axis=0), 'fsdp')]
    dot_general x3 -> x0, matrix products: 30.2 us -> none  [the longest x1 10.7 us: local(): lax.dot_general(columns, key_grad, (((0,), (0,)), ((), ())), preferred_el...]
    unnamed x8 -> x11, local copies, waits for them, and re-layouts: 0.02 us -> 7.15 us
  transfers between devices with their start and end apart: 3 -> 0, of which waited for: 1 -> 0; matrix products, arithmetic and copies ran while one was open for 6% -> 0% of each run, Pallas kernels for 0% -> 0%
where the time goes in v1:
time: 114 us
  Pallas kernels  106 us (93%)
  local copies, waits for them, and re-layouts  7.15 us (6%)
  between operations  1.29 us (1%)
    pallas_call x1, Pallas kernels, local(): pl.pallas_call(kernel, out_shape=(jax.ShapeDtypeStruct((rows, kw), BF16),...  106 us
    unnamed x11, local copies, waits for them, and re-layouts  7.15 us

profile of v1, /device:TPU:1, one launch (start us, length us, event | category | flops | bytes accessed | tf_op | source)
XLA Modules:
  0.0 114.3 jit_solution(6495870360432158653)
XLA Ops:
  1.3 105.9 %outer_and_keys.1 = (bf16[384,512]{1,0:T(8,128)(2,1)}, f32[1024,512]{1,0:T(8,128)}, f32[4,2,8,128]{3,2,1,0:T(8,128)}, f32[16,8192]{1,0:T(8,128)}, f32[16,8192]{1,0:T(8,128)}) custom-call(bf16[384,8192]{1,0:T(8,128)(2,1)} %tok_hbm.1, bf16[1024,512]{1,0:T(8,128)(2,1)} %bitcast.6, bf16[384,512]{1,0:T(8,128)(2,1)} %kg_hbm.1, f32[1,8192]{1,0:T(1,128)} %gain_hbm.1, ...), custom_call_target="tpu_custom_call" | custom-call | flops 9663676416 | bytes 16777216 | tf_op jit(solution)/shard_map/outer_and_keys/pallas_call | solution.py:483
  107.2 1.8 %copy.19 = bf16[384,512]{1,0:T(8,128)(2,1)} copy(bf16[384,512]{1,0:T(8,128)(2,1)} %get-tuple-element.20) | data formatting | bytes 786432
  108.9 0.0 copy-start.2
  108.9 0.0 copy-start.1
  108.9 0.0 copy-start
  108.9 3.2 %copy.20 = f32[1,1024,512]{2,1,0:T(8,128)} copy(f32[1,1024,512]{2,1,0:T(8,128)} %bitcast.4) | data formatting | bytes 4194304
  112.1 0.0 copy-done.2
  112.1 0.6 copy.21
  112.7 0.0 copy-done.1
  112.7 0.8 copy.22
  113.5 0.0 copy-done
  113.5 0.8 copy.23
Async XLA Ops:
  108.9 3.2 %copy-start.2 = (f32[4,2,8,128]{3,2,1,0:T(8,128)S(1)}, f32[4,2,8,128]{3,2,1,0:T(8,128)}, u32[]{:S(2)}) copy-start(f32[4,2,8,128]{3,2,1,0:T(8,128)} %get-tuple-element.12) | copy-start | bytes 98308
  108.9 3.8 %copy-start.1 = (f32[16,8192]{1,0:T(8,128)S(1)}, f32[16,8192]{1,0:T(8,128)}, u32[]{:S(2)}) copy-start(f32[16,8192]{1,0:T(8,128)} %get-tuple-element.23) | copy-start | bytes 1572868
  108.9 4.6 %copy-start = (f32[16,8192]{1,0:T(8,128)S(1)}, f32[16,8192]{1,0:T(8,128)}, u32[]{:S(2)}) copy-start(f32[16,8192]{1,0:T(8,128)} %get-tuple-element.24) | copy-start | bytes 1572868

commit v2 on v1

--- a/solution.py
+++ b/solution.py
@@ -19,7 +19,7 @@
 XS, YS, ZS = 4, 4, 2
 CHUNKS = 4
 STEPS = CHIPS * CHUNKS
-AHEAD = 3
+LAST = STEPS - CHUNKS
 LOADS = 6
 ROWS = 16
 MIB = 1024 * 1024
@@ -30,14 +30,14 @@
 
 def kernel(
     tok_hbm, kw_hbm, kg_hbm, gain_hbm, op_hbm, lp_hbm, mo_hbm, step_ref,
-    keys_hbm, wg_hbm, gg_hbm, no_hbm, nm_hbm,
-    tok, nrm, kg, gain, inv, buf, kacc, kout, wg,
-    g_own, g_sib, g_z, g_fin,
-    xr, ysum, yr, zs, zr, ps, op, mo,
-    tok_sem, ld_sem, out_sem,
+    kout, wg, g_fin, op, mo,
+    tok, nrm, kg, gain, inv, buf, kacc,
+    g_own, g_sib, g_z,
+    xr, ysum, yr, zs, zr, ps,
+    tok_sem, ld_sem,
     r_send, r_recv, l_send, l_recv,
     w_send, w_recv, p_send, p_recv,
-    g_send, g_recv, o_send, o_recv,
+    g_send, g_recv, o_send, o_recv, here_sem,
 ):
     tokens, width = tok.shape
     shard, kw = buf.shape[1:]
@@ -67,6 +67,30 @@
 
     def rows_of(i):
         return pl.ds(pl.multiple_of(i * part, part), part)
+
+    barrier = pltpu.get_barrier_semaphore()
+    partner = at_rep(1 - q, x, y)
+    peers = [sibling]
+    peers += [at_rep(q, lax.rem(x + d, XS), y) for d in range(1, XS)]
+    peers += [at_rep(q, x, lax.rem(y + d, YS)) for d in range(1, YS)]
+
+    def greet(peer):
+        pl.semaphore_signal(barrier, inc=1, device_id=peer, device_id_type=MESH)
+
+    @pl.when(has_right)
+    def _():
+        greet(right)
+
+    @pl.when(has_left)
+    def _():
+        greet(left)
+
+    for peer in peers:
+        greet(peer)
+
+    @pl.when(q == 0)
+    def _():
+        greet(partner)
 
     block = tokens // LOADS
 
@@ -90,14 +114,8 @@
     for load in (load_w, load_lp, load_op, load_mo):
         load.start()
 
-    barrier = pltpu.get_barrier_semaphore()
-    peers = [at_chip(lax.rem(z + d, CHIPS)) for d in range(1, CHIPS)] + [sibling]
-    peers += [at_rep(q, lax.rem(x + d, XS), y) for d in range(1, XS)]
-    peers += [at_rep(q, x, lax.rem(y + d, YS)) for d in range(1, YS)]
-    peers += [at_rep(1 - q, x, y)]
-    for peer in peers:
-        pl.semaphore_signal(barrier, inc=1, device_id=peer, device_id_type=MESH)
-    pl.semaphore_wait(barrier, len(peers))
+    middle = jnp.logical_and(has_left, has_right).astype(jnp.int32)
+    pl.semaphore_wait(barrier, len(peers) + 1 + middle + q)
 
     def line_first(n, rightward):
         rows = rows_of(n)
@@ -169,7 +187,7 @@
         slot = yr.at[lax.rem(y + YS - d, YS)]
         return remote(slot, slot, o_send.at[1, d - 1], o_recv.at[1, d - 1], sibling)
 
-    z_copy = remote(zs, zr, o_send.at[2, 0], o_recv.at[2, 0], at_rep(1 - q, x, y))
+    z_copy = remote(zs, zr, o_send.at[2, 0], o_recv.at[2, 0], partner)
 
     def y_back(d):
         piece = ps.at[x, y]
@@ -193,6 +211,10 @@
 
     for d in range(1, XS):
         x_copy(d).start()
+
+    @pl.when(q == 1)
+    def _():
+        pl.semaphore_signal(here_sem, inc=1, device_id=partner, device_id_type=MESH)
 
     load_gain.wait()
     lanes = 128
@@ -269,25 +291,26 @@
         def _():
             buf[P0 + 2 * j + c, rows, :] = own.astype(BF16)
 
-    def write_rows(i):
-        rows = rows_of(i)
-        return pltpu.make_async_copy(wg.at[rows], wg_hbm.at[rows], out_sem.at[i])
-
-    write_keys = pltpu.make_async_copy(kout, keys_hbm, out_sem.at[CHUNKS])
-    write_gain = pltpu.make_async_copy(g_fin, gg_hbm, out_sem.at[CHUNKS + 1])
-    write_op = pltpu.make_async_copy(op, no_hbm, out_sem.at[CHUNKS + 2])
-    write_mo = pltpu.make_async_copy(mo, nm_hbm, out_sem.at[CHUNKS + 3])
-
     gain_swap = remote(g_own.at[o], g_sib, g_send.at[0], g_recv.at[0], sibling)
 
     def gain_copy(d):
-        return remote(g_z.at[z], g_z.at[z], g_send.at[d], g_recv.at[d], at_chip(lax.rem(z + d, CHIPS)))
+        to = lax.rem(z + d, CHIPS)
+        return remote(g_own.at[c, to], g_z.at[z], g_send.at[d], g_recv.at[d], at_chip(to))
 
     def gain_wait(d):
         slot = g_z.at[lax.rem(z + CHIPS - d, CHIPS)]
         return remote(slot, slot, g_send.at[d], g_recv.at[d], sibling)
 
-    gain_back = remote(g_fin.at[:, c], g_fin.at[:, c], g_send.at[CHIPS], g_recv.at[CHIPS], sibling)
+    def gain_out(d):
+        sem = CHIPS + d - 1
+        return remote(g_fin.at[z, c], g_fin.at[z, c], g_send.at[sem], g_recv.at[sem], at_chip(lax.rem(z + d, CHIPS)))
+
+    def gain_in(d):
+        slot, sem = g_fin.at[lax.rem(z + CHIPS - d, CHIPS), c], CHIPS + d - 1
+        return remote(slot, slot, g_send.at[sem], g_recv.at[sem], sibling)
+
+    gain_back = remote(g_fin.at[:, c], g_fin.at[:, c], g_send.at[2 * CHIPS - 1], g_recv.at[2 * CHIPS - 1], sibling)
+    gain_back_in = remote(g_fin.at[:, o], g_fin.at[:, o], g_send.at[2 * CHIPS - 1], g_recv.at[2 * CHIPS - 1], sibling)
 
     @pl.loop(0, STEPS)
     def _(s):
@@ -315,6 +338,11 @@
             cols = pl.ds(pl.multiple_of(x * xcols + y * ycols, ycols), ycols)
             total = (yr[0] + yr[1]) + (yr[2] + yr[3])
             zs[...] = (float(XS * YS) * op[:, cols] - total).astype(BF16)
+
+            @pl.when(q == 0)
+            def _():
+                pl.semaphore_wait(here_sem, 1)
+
             z_copy.start()
 
         @pl.when(s == 8)
@@ -344,35 +372,48 @@
                     moment = OUTER_MOMENTUM * mo[:, cols] + pseudo
                     mo[:, cols] = moment
                     op[:, cols] = op[:, cols] - rate * (pseudo + OUTER_MOMENTUM * moment)
-            write_op.start()
-            write_mo.start()
-
-        @pl.when(s == STEPS - 1)
+
+        @pl.when(s == LAST)
+        def _():
+            gain_swap.wait_recv()
+            g_own[c] = g_own[c] + g_sib[...]
+            for d in range(1, CHIPS):
+                gain_copy(d).start()
+            g_z[z] = g_own[c, z]
+
+        @pl.when(has_left)
+        def _():
+            line_copy(s, True).wait_recv()
+
+        @pl.when(has_right)
+        def _():
+            line_copy(s, False).wait_recv()
+
+        left_weights = jnp.logical_and(has_left, k <= z - 1)
+        right_weights = jnp.logical_and(has_right, k <= CHIPS - 2 - z)
+
+        @pl.when(left_weights)
+        def _():
+            to_sibling(z - 1 - k, i).start()
+
+        @pl.when(right_weights)
+        def _():
+            to_sibling(z + 1 + k, i).start()
+
+        @pl.when(s == LAST + 1)
         def _():
             for d in range(1, CHIPS):
                 gain_wait(d).wait_recv()
-            g_fin[:, c] = (g_z[0] + g_z[1]) + (g_z[2] + g_z[3])
+            g_fin[z, c] = (g_z[0] + g_z[1]) + (g_z[2] + g_z[3])
+            for d in range(1, CHIPS):
+                gain_out(d).start()
+
+        @pl.when(s == LAST + 2)
+        def _():
+            for d in range(1, CHIPS):
+                gain_in(d).wait_recv()
             gain_back.start()
 
-        @pl.when(has_left)
-        def _():
-            line_copy(s, True).wait_recv()
-
-        @pl.when(has_right)
-        def _():
-            line_copy(s, False).wait_recv()
-
-        left_weights = jnp.logical_and(has_left, k <= z - 1)
-        right_weights = jnp.logical_and(has_right, k <= CHIPS - 2 - z)
-
-        @pl.when(left_weights)
-        def _():
-            to_sibling(z - 1 - k, i).start()
-
-        @pl.when(right_weights)
-        def _():
-            to_sibling(z + 1 + k, i).start()
-
         later = k + 1
 
         @pl.when(jnp.logical_and(has_right, jnp.logical_and(later < CHIPS, later > z)))
@@ -383,13 +424,14 @@
         def _():
             add_terms(later + z - CHIPS, i, L0, has_right)
 
-        n = s + AHEAD
-
-        @pl.when(jnp.logical_and(has_right, jnp.logical_and(n >= CHUNKS, n < STEPS)))
+        n = s + CHUNKS - 2 * (s // LAST)
+        due = jnp.logical_or(s < LAST - 2, jnp.logical_and(s >= LAST, s < LAST + 2))
+
+        @pl.when(jnp.logical_and(has_right, due))
         def _():
             line_copy(n, True).start()
 
-        @pl.when(jnp.logical_and(has_left, jnp.logical_and(n >= CHUNKS, n < STEPS)))
+        @pl.when(jnp.logical_and(has_left, due))
         def _():
             line_copy(n, False).start()
 
@@ -407,36 +449,24 @@
             def _():
                 wg[rows, :] += buf[L0 + z, rows, :].astype(F32)
 
-            write_rows(i).start()
-
-        before = s - 1 + CHUNKS
-        k_before, i_before = before // CHUNKS - 1, before % CHUNKS
-
-        @pl.when(jnp.logical_and(s > 0, jnp.logical_and(has_left, k_before <= z - 1)))
-        def _():
-            use_both(z - 1 - k_before, i_before)
-
-        @pl.when(jnp.logical_and(s > 0, jnp.logical_and(has_right, k_before <= CHIPS - 2 - z)))
-        def _():
-            use_both(z + 1 + k_before, i_before)
+        @pl.when(left_weights)
+        def _():
+            use_both(z - 1 - k, i)
+
+        @pl.when(right_weights)
+        def _():
+            use_both(z + 1 + k, i)
 
         @pl.when(k == 1)
         def _():
             use_both(z, i)
 
-        @pl.when(s == STEPS - CHUNKS)
+        @pl.when(s == LAST - 1)
         def _():
             gain_swap.start()
-            gain_swap.wait_recv()
-            g_z[z] = g_own[c] + g_sib[...]
-            for d in range(1, CHIPS):
-                gain_copy(d).start()
             kout[...] = kacc[...].astype(BF16)
-            write_keys.start()
-
-    gain_back_in = remote(g_fin.at[:, o], g_fin.at[:, o], g_send.at[CHIPS], g_recv.at[CHIPS], sibling)
+
     gain_back_in.wait_recv()
-    write_gain.start()
 
     @pl.when(has_right)
     def _():
@@ -459,6 +489,7 @@
     gain_back.wait_send()
     for d in range(1, CHIPS):
         gain_copy(d).wait_send()
+        gain_out(d).wait_send()
     for d in range(1, XS):
         x_copy(d).wait_send()
         x_back(d).wait_send()
@@ -467,9 +498,14 @@
         y_back(d).wait_send()
     z_copy.wait_send()
 
-    for i in range(CHUNKS):
-        write_rows(i).wait()
-    for write in (write_keys, write_gain, write_op, write_mo):
+
+def write_out(*refs):
+    count = len(refs) // 2
+    results, outs, sems = refs[:count], refs[count : 2 * count], refs[-1]
+    writes = [pltpu.make_async_copy(a, b, sems.at[i]) for i, (a, b) in enumerate(zip(results, outs))]
+    for write in writes:
+        write.start()
+    for write in writes:
         write.wait()
 
 
@@ -479,18 +515,19 @@
     frag = outer_params.shape[0]
     xcols, ycols = width // XS, width // XS // YS
     lanes = 128
-    dma, anywhere = pltpu.SemaphoreType.DMA, pl.BlockSpec(memory_space=pl.ANY)
-    keys, weight_grad, gain_grad, new_outer, new_momentum = pl.pallas_call(
+    dma, anywhere = pltpu.SemaphoreType.DMA, pl.BlockSpec(memory_space=pltpu.HBM)
+    results = (
+        ((rows, kw), BF16),
+        ((shard, kw), F32),
+        ((CHIPS, CORES, shard // lanes, lanes), F32),
+        (outer_params.shape, F32),
+        (momentum.shape, F32),
+    )
+    held = pl.pallas_call(
         kernel,
-        out_shape=(
-            jax.ShapeDtypeStruct((rows, kw), BF16),
-            jax.ShapeDtypeStruct((shard, kw), F32),
-            jax.ShapeDtypeStruct((CHIPS, CORES, shard // lanes, lanes), F32),
-            jax.ShapeDtypeStruct(outer_params.shape, F32),
-            jax.ShapeDtypeStruct(momentum.shape, F32),
-        ),
+        out_shape=tuple(pltpu.VMEM(*result) for result in results),
         in_specs=[anywhere] * 7 + [pl.BlockSpec(memory_space=pltpu.SMEM)],
-        out_specs=(anywhere,) * 5,
+        out_specs=(pl.BlockSpec(memory_space=pltpu.VMEM),) * 5,
         scratch_shapes=[
             pltpu.VMEM((rows, width), BF16),
             pltpu.VMEM((rows, width), BF16),
@@ -499,23 +536,17 @@
             pltpu.VMEM((rows, lanes), F32),
             pltpu.VMEM((SLOTS, shard, kw), BF16),
             pltpu.VMEM((rows, kw), F32),
-            pltpu.VMEM((rows, kw), BF16),
-            pltpu.VMEM((shard, kw), F32),
             pltpu.VMEM((CORES, CHIPS, shard // lanes, lanes), F32),
             pltpu.VMEM((CHIPS, shard // lanes, lanes), F32),
-            pltpu.VMEM((CHIPS, CHIPS, shard // lanes, lanes), F32),
-            pltpu.VMEM((CHIPS, CORES, shard // lanes, lanes), F32),
+            pltpu.VMEM((CHIPS, shard // lanes, lanes), F32),
             pltpu.VMEM((XS, frag, xcols), BF16),
             pltpu.VMEM((YS, frag, ycols), F32),
             pltpu.VMEM((YS, frag, ycols), F32),
             pltpu.VMEM((frag, ycols), BF16),
             pltpu.VMEM((frag, ycols), BF16),
             pltpu.VMEM((XS, YS, frag, ycols), F32),
-            pltpu.VMEM((frag, width), F32),
-            pltpu.VMEM((frag, width), F32),
             dma((LOADS,)),
             dma((6,)),
-            dma((CHUNKS + 4,)),
             dma((STEPS,)),
             dma((STEPS,)),
             dma((STEPS,)),
@@ -524,13 +555,14 @@
             dma((CHIPS, CHUNKS)),
             dma((CHIPS, CHUNKS)),
             dma((CHIPS, CHUNKS)),
-            dma((CHIPS + 1,)),
-            dma((CHIPS + 1,)),
+            dma((2 * CHIPS,)),
+            dma((2 * CHIPS,)),
             dma((5, 3)),
             dma((5, 3)),
+            pltpu.SemaphoreType.REGULAR,
         ],
         compiler_params=pltpu.CompilerParams(
-            collective_id=0, has_side_effects=True, vmem_limit_bytes=60 * MIB
+            collective_id=0, has_side_effects=True, vmem_limit_bytes=54 * MIB
         ),
         cost_estimate=pl.CostEstimate(
             flops=6 * rows * width * kw, bytes_accessed=16 * MIB, transcendentals=rows
@@ -539,6 +571,15 @@
     )(
         tokens, key_weight[0], key_grad, norm_gain, outer_params, local_params[0], momentum, outer_step
     )
+    keys, weight_grad, gain_grad, new_outer, new_momentum = pl.pallas_call(
+        write_out,
+        out_shape=tuple(jax.ShapeDtypeStruct(*result) for result in results),
+        in_specs=[pl.BlockSpec(memory_space=pltpu.VMEM)] * len(results),
+        out_specs=(anywhere,) * len(results),
+        scratch_shapes=[dma((len(results),))],
+        compiler_params=pltpu.CompilerParams(vmem_limit_bytes=MIB),
+        name="write_out",
+    )(*[pltpu.with_memory_space_constraint(a, pltpu.VMEM) for a in held])
     return keys, weight_grad[None], gain_grad.reshape(1, width), new_outer, new_momentum
 
 

time: 114 us -> 103 us (0.904)
  local copies, waits for them, and re-layouts: 7.15 us -> 0 us
  Pallas kernels: 106 us -> 101 us
    unnamed x11 -> x0, local copies, waits for them, and re-layouts: 7.15 us -> none
    pallas_call x1 -> x2, Pallas kernels: 106 us -> 101 us  [the longest x1 99.3 us: local(): pl.pallas_call(kernel, out_shape=tuple((pltpu.VMEM(*result) for result in...]
where the time goes in v2:
time: 103 us; the launch traced here: 102 us
  Pallas kernels  101 us (98%)
  between operations  1.29 us (1%)
    pallas_call x1, Pallas kernels, local(): pl.pallas_call(kernel, out_shape=tuple((pltpu.VMEM(*result) for result in...  99.3 us

profile of v2, /device:TPU:1, one launch (start us, length us, event | category | flops | bytes accessed | tf_op | source)
XLA Modules:
  0.0 102.5 jit_solution(4221393699462364543)
XLA Ops:
  1.3 99.3 %outer_and_keys.1 = (bf16[384,512]{1,0:T(8,128)(2,1)S(1)}, f32[1024,512]{1,0:T(8,128)S(1)}, f32[4,2,8,128]{3,2,1,0:T(8,128)S(1)}, f32[16,8192]{1,0:T(8,128)S(1)}, f32[16,8192]{1,0:T(8,128)S(1)}) custom-call(bf16[384,8192]{1,0:T(8,128)(2,1)} %tok_hbm.1, bf16[1024,512]{1,0:T(8,128)(2,1)} %bitcast.5, bf16[384,512]{1,0:T(8,128)(2,1)} %kg_hbm.1, ...), custom_call_target="tpu_custom_call" | custom-call | flops 9663676416 | bytes 16777216 | tf_op jit(solution)/shard_map/outer_and_keys/pallas_call | solution.py:526
  100.6 1.8 %write_out.1 = (bf16[384,512]{1,0:T(8,128)(2,1)}, f32[1024,512]{1,0:T(8,128)}, f32[4,2,8,128]{3,2,1,0:T(8,128)}, f32[16,8192]{1,0:T(8,128)}, f32[16,8192]{1,0:T(8,128)}) custom-call(bf16[384,512]{1,0:T(8,128)(2,1)S(1)} %get-tuple-element.15.refs_0_, f32[1024,512]{1,0:T(8,128)S(1)} %get-tuple-element.16.refs_1_, ...), custom_call_target="tpu_custom_call" | custom-call | tf_op jit(solution)/shard_map/write_out/pallas_call | solution.py:574

commit v3 on v2

--- a/solution.py
+++ b/solution.py
@@ -22,6 +22,7 @@
 LAST = STEPS - CHUNKS
 LOADS = 6
 ROWS = 16
+PIECES = (1, 1, 1, 1, 1)
 MIB = 1024 * 1024
 
 W0, P0, S0, R0, L0 = 0, 8, 16, 20, 24
@@ -29,15 +30,15 @@
 
 
 def kernel(
-    tok_hbm, kw_hbm, kg_hbm, gain_hbm, op_hbm, lp_hbm, mo_hbm, step_ref,
+    tok_hbm, kw_hbm, kg_hbm, gain_hbm, op_hbm, lp_hbm, mo_hbm, step_hbm,
     kout, wg, g_fin, op, mo,
     tok, nrm, kg, gain, inv, buf, kacc,
     g_own, g_sib, g_z,
     xr, ysum, yr, zs, zr, ps,
-    tok_sem, ld_sem,
+    step_ref, tok_sem, ld_sem,
     r_send, r_recv, l_send, l_recv,
     w_send, w_recv, p_send, p_recv,
-    g_send, g_recv, o_send, o_recv, here_sem,
+    g_send, g_recv, o_send, o_recv, here_sem, line_sem, all_sem,
 ):
     tokens, width = tok.shape
     shard, kw = buf.shape[1:]
@@ -70,27 +71,52 @@
 
     barrier = pltpu.get_barrier_semaphore()
     partner = at_rep(1 - q, x, y)
-    peers = [sibling]
-    peers += [at_rep(q, lax.rem(x + d, XS), y) for d in range(1, XS)]
-    peers += [at_rep(q, x, lax.rem(y + d, YS)) for d in range(1, YS)]
 
     def greet(peer):
         pl.semaphore_signal(barrier, inc=1, device_id=peer, device_id_type=MESH)
 
+    def answer(peer):
+        pl.semaphore_signal(here_sem, inc=1, device_id=peer, device_id_type=MESH)
+
+    def wait_for(sem, count):
+        @pl.when(count > 0)
+        def _():
+            pl.semaphore_wait(sem, count)
+
+    both = jnp.logical_and(has_right, q == 1)
+
     @pl.when(has_right)
     def _():
         greet(right)
 
-    @pl.when(has_left)
+    @pl.when(jnp.logical_and(has_left, q == 1))
     def _():
         greet(left)
 
-    for peer in peers:
-        greet(peer)
+    @pl.when(c == 1)
+    def _():
+        greet(sibling)
+
+    @pl.when(x == 0)
+    def _():
+        for d in range(1, XS):
+            greet(at_rep(q, d, y))
+
+    @pl.when(y == 0)
+    def _():
+        for d in range(1, YS):
+            greet(at_rep(q, x, d))
 
     @pl.when(q == 0)
     def _():
         greet(partner)
+
+    x_later, y_later = (x > 0).astype(jnp.int32), (y > 0).astype(jnp.int32)
+    wait_for(barrier, has_left.astype(jnp.int32) + both.astype(jnp.int32) + o + x_later + y_later + q)
+
+    @pl.when(jnp.logical_and(has_left, q == 0))
+    def _():
+        pl.semaphore_signal(line_sem, inc=1, device_id=left, device_id_type=MESH)
 
     block = tokens // LOADS
 
@@ -105,17 +131,7 @@
     load_lp = pltpu.make_async_copy(lp_hbm.at[:, own_x], xr.at[x], ld_sem.at[3])
     load_op = pltpu.make_async_copy(op_hbm, op, ld_sem.at[4])
     load_mo = pltpu.make_async_copy(mo_hbm, mo, ld_sem.at[5])
-
-    load_gain.start()
-    tok_load(0).start()
-    load_kg.start()
-    for b in range(1, LOADS):
-        tok_load(b).start()
-    for load in (load_w, load_lp, load_op, load_mo):
-        load.start()
-
-    middle = jnp.logical_and(has_left, has_right).astype(jnp.int32)
-    pl.semaphore_wait(barrier, len(peers) + 1 + middle + q)
+    load_step = pltpu.make_async_copy(step_hbm, step_ref, ld_sem.at[6])
 
     def line_first(n, rightward):
         rows = rows_of(n)
@@ -138,15 +154,27 @@
         dst = (1 - is_sum) * (W0 + weight) + is_sum * (L0 + owner)
         return remote(buf.at[src, rows], buf.at[dst, rows], l_send.at[n], l_recv.at[n], left)
 
-    for n in range(CHUNKS):
-
-        @pl.when(has_right)
-        def _():
+    @pl.when(has_left)
+    def _():
+        for n in range(CHUNKS):
+            line_first(n, False).start()
+
+    @pl.when(jnp.logical_and(has_right, q == 0))
+    def _():
+        pl.semaphore_wait(line_sem, 1)
+
+    @pl.when(has_right)
+    def _():
+        for n in range(CHUNKS):
             line_first(n, True).start()
 
-        @pl.when(has_left)
-        def _():
-            line_first(n, False).start()
+    load_gain.start()
+    tok_load(0).start()
+    load_kg.start()
+    for b in range(1, LOADS):
+        tok_load(b).start()
+    for load in (load_w, load_lp, load_op, load_mo, load_step):
+        load.start()
 
     def own_to_sibling(i):
         rows = rows_of(i)
@@ -167,9 +195,6 @@
             buf.at[P0 + 2 * j + o, rows_of(i)], buf.at[S0 + j, rows_of(i)], p_send.at[j, i], p_recv.at[j, i], sibling
         )
 
-    for i in range(CHUNKS):
-        own_to_sibling(i).start()
-
     def x_copy(d):
         to = lax.rem(x + d, XS)
         cols = pl.ds(pl.multiple_of(to * xcols, xcols), xcols)
@@ -209,12 +234,21 @@
         piece = ps.at[lax.rem(x + XS - d, XS)]
         return remote(piece, piece, o_send.at[4, d - 1], o_recv.at[4, d - 1], sibling)
 
-    for d in range(1, XS):
-        x_copy(d).start()
+    @pl.when(x > 0)
+    def _():
+        answer(at_rep(q, 0, y))
+
+    @pl.when(y > 0)
+    def _():
+        answer(at_rep(q, x, 0))
 
     @pl.when(q == 1)
     def _():
-        pl.semaphore_signal(here_sem, inc=1, device_id=partner, device_id_type=MESH)
+        answer(partner)
+
+    @pl.when(c == 0)
+    def _():
+        answer(sibling)
 
     load_gain.wait()
     lanes = 128
@@ -238,6 +272,21 @@
                 cols = slice(m * lanes, (m + 1) * lanes)
                 nrm[rows, cols] = (tok[rows, cols].astype(F32) * scale * gain[:, cols]).astype(BF16)
 
+    wait_for(here_sem, (1 - x_later) * (XS - 1) + (1 - y_later) * (YS - 1) + (ZS - 1 - q) + c)
+
+    @pl.when(x == 0)
+    def _():
+        for d in range(1, XS):
+            pl.semaphore_signal(all_sem, inc=1, device_id=at_rep(q, d, y), device_id_type=MESH)
+
+    @pl.when(y == 0)
+    def _():
+        for d in range(1, YS):
+            pl.semaphore_signal(all_sem, inc=1, device_id=at_rep(q, x, d), device_id_type=MESH)
+
+    for i in range(CHUNKS):
+        own_to_sibling(i).start()
+
     load_kg.wait()
     upper = z // (CHIPS // 2)
 
@@ -257,6 +306,10 @@
         terms(2 * j + o, i)
         terms_to_sibling(j, i).start()
         terms(2 * j + c, i)
+
+    wait_for(all_sem, x_later + y_later)
+    for d in range(1, XS):
+        x_copy(d).start()
 
     kacc[...] = jnp.zeros_like(kacc)
     load_w.wait()
@@ -330,7 +383,7 @@
                 y_copy(d).start()
             yr[y] = ysum[y]
 
-        @pl.when(s == 3)
+        @pl.when(s == 4)
         def _():
             for d in range(1, YS):
                 y_wait(d).wait_recv()
@@ -338,32 +391,28 @@
             cols = pl.ds(pl.multiple_of(x * xcols + y * ycols, ycols), ycols)
             total = (yr[0] + yr[1]) + (yr[2] + yr[3])
             zs[...] = (float(XS * YS) * op[:, cols] - total).astype(BF16)
-
-            @pl.when(q == 0)
-            def _():
-                pl.semaphore_wait(here_sem, 1)
-
             z_copy.start()
 
-        @pl.when(s == 8)
+        @pl.when(s == 9)
         def _():
             z_copy.wait_recv()
             ps[x, y] = (zs[...].astype(F32) + zr[...].astype(F32)) * (1.0 / (XS * YS * ZS))
             for d in range(1, YS):
                 y_back(d).start()
 
-        @pl.when(s == 9)
+        @pl.when(s == 10)
         def _():
             for d in range(1, YS):
                 y_back_wait(d).wait_recv()
             for d in range(1, XS):
                 x_back(d).start()
 
-        @pl.when(s == 10)
+        @pl.when(s == STEPS - 2)
         def _():
             for d in range(1, XS):
                 x_back_wait(d).wait_recv()
             load_mo.wait()
+            load_step.wait()
             rate = OUTER_LR * (step_ref[0].astype(F32) + 1.0) / WARM
             for a in range(XS):
                 for b in range(YS):
@@ -373,7 +422,104 @@
                     mo[:, cols] = moment
                     op[:, cols] = op[:, cols] - rate * (pseudo + OUTER_MOMENTUM * moment)
 
-        @pl.when(s == LAST)
+        @pl.when(s == LAST + 1)
+        def _():
+            for d in range(1, CHIPS):
+                gain_wait(d).wait_recv()
+            g_fin[z, c] = (g_z[0] + g_z[1]) + (g_z[2] + g_z[3])
+            for d in range(1, CHIPS):
+                gain_out(d).start()
+
+        @pl.when(s == STEPS - 1)
+        def _():
+            for d in range(1, CHIPS):
+                gain_in(d).wait_recv()
+            gain_back.start()
+
+        @pl.when(jnp.logical_and(has_right, s > 1))
+        def _():
+            line_copy(s - 2, True).wait_send()
+
+        @pl.when(jnp.logical_and(has_left, s > 1))
+        def _():
+            line_copy(s - 2, False).wait_send()
+
+        @pl.when(k == CHIPS - 1)
+        def _():
+            for a in range(CHIPS):
+                to_sibling(a, i).wait_send()
+                terms_to_sibling(a, i).wait_send()
+
+        @pl.when(s == LAST + 1)
+        def _():
+            gain_swap.wait_send()
+            for d in range(1, XS):
+                x_copy(d).wait_send()
+                x_back(d).wait_send()
+            for d in range(1, YS):
+                y_copy(d).wait_send()
+                y_back(d).wait_send()
+            z_copy.wait_send()
+
+        @pl.when(s == STEPS - 1)
+        def _():
+            for d in range(1, CHIPS):
+                gain_copy(d).wait_send()
+                gain_out(d).wait_send()
+
+        @pl.when(k == CHIPS - 1)
+        def _():
+            rows = rows_of(i)
+            terms_to_sibling(z, i).wait_recv()
+            wg[rows, :] = buf[P0 + 2 * z + c, rows, :].astype(F32) + buf[S0 + z, rows, :].astype(F32)
+
+        @pl.when(has_left)
+        def _():
+            line_copy(s, True).wait_recv()
+
+        @pl.when(has_right)
+        def _():
+            line_copy(s, False).wait_recv()
+
+        left_weights = jnp.logical_and(has_left, k <= z - 1)
+        right_weights = jnp.logical_and(has_right, k <= CHIPS - 2 - z)
+
+        @pl.when(left_weights)
+        def _():
+            to_sibling(z - 1 - k, i).start()
+
+        @pl.when(right_weights)
+        def _():
+            to_sibling(z + 1 + k, i).start()
+
+        @pl.when(left_weights)
+        def _():
+            use_both(z - 1 - k, i)
+
+        @pl.when(right_weights)
+        def _():
+            use_both(z + 1 + k, i)
+
+        @pl.when(k == 1)
+        def _():
+            use_both(z, i)
+
+        @pl.when(s == LAST - 1)
+        def _():
+            gain_swap.start()
+            kout[...] = kacc[...].astype(BF16)
+
+        later = k + 1
+
+        @pl.when(jnp.logical_and(has_right, jnp.logical_and(later < CHIPS, later > z)))
+        def _():
+            add_terms(CHIPS + z - later, i, R0, has_left)
+
+        @pl.when(jnp.logical_and(has_left, jnp.logical_and(later < CHIPS, later > CHIPS - 1 - z)))
+        def _():
+            add_terms(later + z - CHIPS, i, L0, has_right)
+
+        @pl.when(s == LAST - 1)
         def _():
             gain_swap.wait_recv()
             g_own[c] = g_own[c] + g_sib[...]
@@ -381,51 +527,9 @@
                 gain_copy(d).start()
             g_z[z] = g_own[c, z]
 
-        @pl.when(has_left)
-        def _():
-            line_copy(s, True).wait_recv()
-
-        @pl.when(has_right)
-        def _():
-            line_copy(s, False).wait_recv()
-
-        left_weights = jnp.logical_and(has_left, k <= z - 1)
-        right_weights = jnp.logical_and(has_right, k <= CHIPS - 2 - z)
-
-        @pl.when(left_weights)
-        def _():
-            to_sibling(z - 1 - k, i).start()
-
-        @pl.when(right_weights)
-        def _():
-            to_sibling(z + 1 + k, i).start()
-
-        @pl.when(s == LAST + 1)
-        def _():
-            for d in range(1, CHIPS):
-                gain_wait(d).wait_recv()
-            g_fin[z, c] = (g_z[0] + g_z[1]) + (g_z[2] + g_z[3])
-            for d in range(1, CHIPS):
-                gain_out(d).start()
-
-        @pl.when(s == LAST + 2)
-        def _():
-            for d in range(1, CHIPS):
-                gain_in(d).wait_recv()
-            gain_back.start()
-
-        later = k + 1
-
-        @pl.when(jnp.logical_and(has_right, jnp.logical_and(later < CHIPS, later > z)))
-        def _():
-            add_terms(CHIPS + z - later, i, R0, has_left)
-
-        @pl.when(jnp.logical_and(has_left, jnp.logical_and(later < CHIPS, later > CHIPS - 1 - z)))
-        def _():
-            add_terms(later + z - CHIPS, i, L0, has_right)
-
-        n = s + CHUNKS - 2 * (s // LAST)
-        due = jnp.logical_or(s < LAST - 2, jnp.logical_and(s >= LAST, s < LAST + 2))
+        early, late = s < LAST + 1 - CHUNKS, jnp.logical_and(s >= LAST - 1, s < LAST + 2)
+        n = s + CHUNKS - (CHUNKS - 2) * late.astype(jnp.int32)
+        due = jnp.logical_or(early, late)
 
         @pl.when(jnp.logical_and(has_right, due))
         def _():
@@ -435,74 +539,37 @@
         def _():
             line_copy(n, False).start()
 
-        @pl.when(k == CHIPS - 1)
-        def _():
-            rows = rows_of(i)
-            terms_to_sibling(z, i).wait_recv()
-            wg[rows, :] = buf[P0 + 2 * z + c, rows, :].astype(F32) + buf[S0 + z, rows, :].astype(F32)
-
-            @pl.when(has_left)
-            def _():
-                wg[rows, :] += buf[R0 + z, rows, :].astype(F32)
-
-            @pl.when(has_right)
-            def _():
-                wg[rows, :] += buf[L0 + z, rows, :].astype(F32)
-
-        @pl.when(left_weights)
-        def _():
-            use_both(z - 1 - k, i)
-
-        @pl.when(right_weights)
-        def _():
-            use_both(z + 1 + k, i)
-
-        @pl.when(k == 1)
-        def _():
-            use_both(z, i)
-
-        @pl.when(s == LAST - 1)
-        def _():
-            gain_swap.start()
-            kout[...] = kacc[...].astype(BF16)
+        @pl.when(jnp.logical_and(has_left, k == CHIPS - 1))
+        def _():
+            wg[rows_of(i), :] += buf[R0 + z, rows_of(i), :].astype(F32)
+
+        @pl.when(jnp.logical_and(has_right, k == CHIPS - 1))
+        def _():
+            wg[rows_of(i), :] += buf[L0 + z, rows_of(i), :].astype(F32)
 
     gain_back_in.wait_recv()
+    gain_back.wait_send()
 
     @pl.when(has_right)
     def _():
-        @pl.loop(0, STEPS)
-        def _(n):
-            line_copy(n, True).wait_send()
+        line_copy(STEPS - 2, True).wait_send()
+        line_copy(STEPS - 1, True).wait_send()
 
     @pl.when(has_left)
     def _():
-        @pl.loop(0, STEPS)
-        def _(n):
-            line_copy(n, False).wait_send()
-
-    @pl.loop(0, STEPS)
-    def _(t):
-        to_sibling(t // CHUNKS, t % CHUNKS).wait_send()
-        terms_to_sibling(t // CHUNKS, t % CHUNKS).wait_send()
-
-    gain_swap.wait_send()
-    gain_back.wait_send()
-    for d in range(1, CHIPS):
-        gain_copy(d).wait_send()
-        gain_out(d).wait_send()
-    for d in range(1, XS):
-        x_copy(d).wait_send()
-        x_back(d).wait_send()
-    for d in range(1, YS):
-        y_copy(d).wait_send()
-        y_back(d).wait_send()
-    z_copy.wait_send()
+        line_copy(STEPS - 2, False).wait_send()
+        line_copy(STEPS - 1, False).wait_send()
 
 
 def write_out(*refs):
-    count = len(refs) // 2
+    count = len(PIECES)
     results, outs, sems = refs[:count], refs[count : 2 * count], refs[-1]
-    writes = [pltpu.make_async_copy(a, b, sems.at[i]) for i, (a, b) in enumerate(zip(results, outs))]
+    writes = []
+    for result, out, pieces in zip(results, outs, PIECES):
+        size = result.shape[0] // pieces
+        for i in range(pieces):
+            here = pl.ds(i * size, size)
+            writes.append(pltpu.make_async_copy(result.at[here], out.at[here], sems.at[len(writes)]))
     for write in writes:
         write.start()
     for write in writes:
@@ -526,7 +593,7 @@
     held = pl.pallas_call(
         kernel,
         out_shape=tuple(pltpu.VMEM(*result) for result in results),
-        in_specs=[anywhere] * 7 + [pl.BlockSpec(memory_space=pltpu.SMEM)],
+        in_specs=[anywhere] * 8,
         out_specs=(pl.BlockSpec(memory_space=pltpu.VMEM),) * 5,
         scratch_shapes=[
             pltpu.VMEM((rows, width), BF16),
@@ -545,8 +612,9 @@
             pltpu.VMEM((frag, ycols), BF16),
             pltpu.VMEM((frag, ycols), BF16),
             pltpu.VMEM((XS, YS, frag, ycols), F32),
+            pltpu.SMEM((1,), jnp.int32),
             dma((LOADS,)),
-            dma((6,)),
+            dma((7,)),
             dma((STEPS,)),
             dma((STEPS,)),
             dma((STEPS,)),
@@ -559,6 +627,8 @@
             dma((2 * CHIPS,)),
             dma((5, 3)),
             dma((5, 3)),
+            pltpu.SemaphoreType.REGULAR,
+            pltpu.SemaphoreType.REGULAR,
             pltpu.SemaphoreType.REGULAR,
         ],
         compiler_params=pltpu.CompilerParams(
@@ -576,7 +646,7 @@
         out_shape=tuple(jax.ShapeDtypeStruct(*result) for result in results),
         in_specs=[pl.BlockSpec(memory_space=pltpu.VMEM)] * len(results),
         out_specs=(anywhere,) * len(results),
-        scratch_shapes=[dma((len(results),))],
+        scratch_shapes=[dma((sum(PIECES),))],
         compiler_params=pltpu.CompilerParams(vmem_limit_bytes=MIB),
         name="write_out",
     )(*[pltpu.with_memory_space_constraint(a, pltpu.VMEM) for a in held])

time: 103 us -> 100 us (0.971)
  Pallas kernels: 101 us -> 98.6 us
    pallas_call x1, Pallas kernels: 99.3 us -> 96.8 us  [local(): pl.pallas_call(kernel, out_shape=tuple((pltpu.VMEM(*result) for result in...]
where the time goes in v3:
time: 100 us; the launch traced here: 99.9 us
  Pallas kernels  98.6 us (99%)
  between operations  1.29 us (1%)
    pallas_call x1, Pallas kernels, local(): pl.pallas_call(kernel, out_shape=tuple((pltpu.VMEM(*result) for result in...  96.8 us

profile of v3, /device:TPU:1, one launch (start us, length us, event | category | flops | bytes accessed | tf_op | source)
XLA Modules:
  0.0 99.9 jit_solution(7028132733515037450)
XLA Ops:
  1.3 96.8 %outer_and_keys.1 = (bf16[384,512]{1,0:T(8,128)(2,1)S(1)}, f32[1024,512]{1,0:T(8,128)S(1)}, f32[4,2,8,128]{3,2,1,0:T(8,128)S(1)}, f32[16,8192]{1,0:T(8,128)S(1)}, f32[16,8192]{1,0:T(8,128)S(1)}) custom-call(bf16[384,8192]{1,0:T(8,128)(2,1)} %tok_hbm.1, bf16[1024,512]{1,0:T(8,128)(2,1)} %bitcast.5, bf16[384,512]{1,0:T(8,128)(2,1)} %kg_hbm.1, ...), custom_call_target="tpu_custom_call" | custom-call | flops 9663676416 | bytes 16777216 | tf_op jit(solution)/shard_map/outer_and_keys/pallas_call | solution.py:593
  98.0 1.8 %write_out.1 = (bf16[384,512]{1,0:T(8,128)(2,1)}, f32[1024,512]{1,0:T(8,128)}, f32[4,2,8,128]{3,2,1,0:T(8,128)}, f32[16,8192]{1,0:T(8,128)}, f32[16,8192]{1,0:T(8,128)}) custom-call(bf16[384,512]{1,0:T(8,128)(2,1)S(1)} %get-tuple-element.15.refs_0_, f32[1024,512]{1,0:T(8,128)S(1)} %get-tuple-element.16.refs_1_, ...), custom_call_target="tpu_custom_call" | custom-call | tf_op jit(solution)/shard_map/write_out/pallas_call | solution.py:644

commit v4 on v3

--- a/solution.py
+++ b/solution.py
@@ -303,9 +303,14 @@
     def _(t):
         n, i = t // CHUNKS, t % CHUNKS
         j = (1 - upper) * (CHIPS - 1 - n) + upper * n
-        terms(2 * j + o, i)
-        terms_to_sibling(j, i).start()
-        terms(2 * j + c, i)
+
+        @pl.loop(0, CORES)
+        def _(turn):
+            terms(2 * j + lax.rem(o + turn, CORES), i)
+
+            @pl.when(turn == 0)
+            def _():
+                terms_to_sibling(j, i).start()
 
     wait_for(all_sem, x_later + y_later)
     for d in range(1, XS):
@@ -325,11 +330,6 @@
             here = slice(m * lanes, (m + 1) * lanes)
             got = jnp.sum(d_normed[:, here] * wide[:, here] * inv[...], axis=0, keepdims=True)
             g_own[core, a, pl.ds(i * (part // lanes) + m, 1), :] = got
-
-    def use_both(a, i):
-        use_rows(a, c, i)
-        from_sibling(a, i).wait_recv()
-        use_rows(a, o, i)
 
     def add_terms(j, i, base, from_line):
         rows = rows_of(i)
@@ -492,17 +492,23 @@
         def _():
             to_sibling(z + 1 + k, i).start()
 
-        @pl.when(left_weights)
-        def _():
-            use_both(z - 1 - k, i)
-
-        @pl.when(right_weights)
-        def _():
-            use_both(z + 1 + k, i)
-
-        @pl.when(k == 1)
-        def _():
-            use_both(z, i)
+        @pl.loop(0, 3 * CORES)
+        def _(t):
+            source, turn = t // CORES, t % CORES
+            is_left, is_right, is_own = source == 0, source == 1, source == 2
+            a = z + (1 + k) * (is_right.astype(jnp.int32) - is_left.astype(jnp.int32))
+            have = jnp.logical_or(
+                jnp.logical_or(jnp.logical_and(is_left, left_weights), jnp.logical_and(is_right, right_weights)),
+                jnp.logical_and(is_own, k == 1),
+            )
+
+            @pl.when(jnp.logical_and(have, turn == 1))
+            def _():
+                from_sibling(a, i).wait_recv()
+
+            @pl.when(have)
+            def _():
+                use_rows(a, lax.rem(c + turn, CORES), i)
 
         @pl.when(s == LAST - 1)
         def _():
@@ -511,13 +517,19 @@
 
         later = k + 1
 
-        @pl.when(jnp.logical_and(has_right, jnp.logical_and(later < CHIPS, later > z)))
-        def _():
-            add_terms(CHIPS + z - later, i, R0, has_left)
-
-        @pl.when(jnp.logical_and(has_left, jnp.logical_and(later < CHIPS, later > CHIPS - 1 - z)))
-        def _():
-            add_terms(later + z - CHIPS, i, L0, has_right)
+        @pl.loop(0, 2)
+        def _(t):
+            to_left = t == 1
+            j = later * (2 * t - 1) + CHIPS * (1 - 2 * t) + z
+            goes = jnp.logical_or(
+                jnp.logical_and(jnp.logical_not(to_left), jnp.logical_and(has_right, later > z)),
+                jnp.logical_and(to_left, jnp.logical_and(has_left, later > CHIPS - 1 - z)),
+            )
+            comes = jnp.logical_or(jnp.logical_and(to_left, has_right), jnp.logical_and(jnp.logical_not(to_left), has_left))
+
+            @pl.when(jnp.logical_and(later < CHIPS, goes))
+            def _():
+                add_terms(j, i, R0 + (L0 - R0) * t, comes)
 
         @pl.when(s == LAST - 1)
         def _():
@@ -527,7 +539,7 @@
                 gain_copy(d).start()
             g_z[z] = g_own[c, z]
 
-        early, late = s < LAST + 1 - CHUNKS, jnp.logical_and(s >= LAST - 1, s < LAST + 2)
+        early, late = s < LAST + 2 - CHUNKS, jnp.logical_and(s >= LAST, s < LAST + 2)
         n = s + CHUNKS - (CHUNKS - 2) * late.astype(jnp.int32)
         due = jnp.logical_or(early, late)
 
@@ -539,13 +551,17 @@
         def _():
             line_copy(n, False).start()
 
-        @pl.when(jnp.logical_and(has_left, k == CHIPS - 1))
-        def _():
-            wg[rows_of(i), :] += buf[R0 + z, rows_of(i), :].astype(F32)
-
-        @pl.when(jnp.logical_and(has_right, k == CHIPS - 1))
-        def _():
-            wg[rows_of(i), :] += buf[L0 + z, rows_of(i), :].astype(F32)
+        @pl.when(k == CHIPS - 1)
+        def _():
+            rows = rows_of(i)
+
+            @pl.when(jnp.logical_and(has_left, has_right))
+            def _():
+                wg[rows, :] += buf[R0 + z, rows, :].astype(F32) + buf[L0 + z, rows, :].astype(F32)
+
+            @pl.when(jnp.logical_not(jnp.logical_and(has_left, has_right)))
+            def _():
+                wg[rows, :] += buf[R0 + z + (L0 - R0) * (1 - has_left.astype(jnp.int32)), rows, :].astype(F32)
 
     gain_back_in.wait_recv()
     gain_back.wait_send()

time: 100 us -> 99.6 us (level)
  no operation moved by 1% of the time
where the time goes in v4:
time: 99.6 us; the launch traced here: 99.4 us
  Pallas kernels  98.1 us (98%)
  between operations  1.29 us (1%)
    pallas_call x1, Pallas kernels, local(): pl.pallas_call(kernel, out_shape=tuple((pltpu.VMEM(*result) for result in...  96.3 us

profile of v4, /device:TPU:1, one launch (start us, length us, event | category | flops | bytes accessed | tf_op | source)
XLA Modules:
  0.0 99.4 jit_solution(3453375810879265950)
XLA Ops:
  1.3 96.3 %outer_and_keys.1 = (bf16[384,512]{1,0:T(8,128)(2,1)S(1)}, f32[1024,512]{1,0:T(8,128)S(1)}, f32[4,2,8,128]{3,2,1,0:T(8,128)S(1)}, f32[16,8192]{1,0:T(8,128)S(1)}, f32[16,8192]{1,0:T(8,128)S(1)}) custom-call(bf16[384,8192]{1,0:T(8,128)(2,1)} %tok_hbm.1, bf16[1024,512]{1,0:T(8,128)(2,1)} %bitcast.5, bf16[384,512]{1,0:T(8,128)(2,1)} %kg_hbm.1, ...), custom_call_target="tpu_custom_call" | custom-call | flops 9663676416 | bytes 16777216 | tf_op jit(solution)/shard_map/outer_and_keys/pallas_call | solution.py:609
  97.6 1.8 %write_out.1 = (bf16[384,512]{1,0:T(8,128)(2,1)}, f32[1024,512]{1,0:T(8,128)}, f32[4,2,8,128]{3,2,1,0:T(8,128)}, f32[16,8192]{1,0:T(8,128)}, f32[16,8192]{1,0:T(8,128)}) custom-call(bf16[384,512]{1,0:T(8,128)(2,1)S(1)} %get-tuple-element.15.refs_0_, f32[1024,512]{1,0:T(8,128)S(1)} %get-tuple-element.16.refs_1_, ...), custom_call_target="tpu_custom_call" | custom-call | tf_op jit(solution)/shard_map/write_out/pallas_call | solution.py:660

commit v5 on v4

--- a/solution.py
+++ b/solution.py
@@ -85,6 +85,10 @@
 
     both = jnp.logical_and(has_right, q == 1)
 
+    @pl.when(q == 0)
+    def _():
+        greet(partner)
+
     @pl.when(has_right)
     def _():
         greet(right)
@@ -106,10 +110,6 @@
     def _():
         for d in range(1, YS):
             greet(at_rep(q, x, d))
-
-    @pl.when(q == 0)
-    def _():
-        greet(partner)
 
     x_later, y_later = (x > 0).astype(jnp.int32), (y > 0).astype(jnp.int32)
     wait_for(barrier, has_left.astype(jnp.int32) + both.astype(jnp.int32) + o + x_later + y_later + q)

time: 99.6 us -> 99.6 us (level)
  no operation moved by 1% of the time
where the time goes in v5:
time: 99.6 us; the launch traced here: 99.4 us
  Pallas kernels  98.1 us (98%)
  between operations  1.29 us (1%)
    pallas_call x1, Pallas kernels, local(): pl.pallas_call(kernel, out_shape=tuple((pltpu.VMEM(*result) for result in...  96.3 us

profile of v5, /device:TPU:1, one launch (start us, length us, event | category | flops | bytes accessed | tf_op | source)
XLA Modules:
  0.0 99.4 jit_solution(17674673665831041308)
XLA Ops:
  1.3 96.3 %outer_and_keys.1 = (bf16[384,512]{1,0:T(8,128)(2,1)S(1)}, f32[1024,512]{1,0:T(8,128)S(1)}, f32[4,2,8,128]{3,2,1,0:T(8,128)S(1)}, f32[16,8192]{1,0:T(8,128)S(1)}, f32[16,8192]{1,0:T(8,128)S(1)}) custom-call(bf16[384,8192]{1,0:T(8,128)(2,1)} %tok_hbm.1, bf16[1024,512]{1,0:T(8,128)(2,1)} %bitcast.5, bf16[384,512]{1,0:T(8,128)(2,1)} %kg_hbm.1, ...), custom_call_target="tpu_custom_call" | custom-call | flops 9663676416 | bytes 16777216 | tf_op jit(solution)/shard_map/outer_and_keys/pallas_call | solution.py:609
  97.6 1.8 %write_out.1 = (bf16[384,512]{1,0:T(8,128)(2,1)}, f32[1024,512]{1,0:T(8,128)}, f32[4,2,8,128]{3,2,1,0:T(8,128)}, f32[16,8192]{1,0:T(8,128)}, f32[16,8192]{1,0:T(8,128)}) custom-call(bf16[384,512]{1,0:T(8,128)(2,1)S(1)} %get-tuple-element.15.refs_0_, f32[1024,512]{1,0:T(8,128)S(1)} %get-tuple-element.16.refs_1_, ...), custom_call_target="tpu_custom_call" | custom-call | tf_op jit(solution)/shard_map/write_out/pallas_call | solution.py:660

commit v6 on v5

--- a/solution.py
+++ b/solution.py
@@ -103,13 +103,21 @@
 
     @pl.when(x == 0)
     def _():
-        for d in range(1, XS):
-            greet(at_rep(q, d, y))
+        greet(at_rep(q, 1, y))
+        greet(at_rep(q, 3, y))
+
+    @pl.when(x == 1)
+    def _():
+        greet(at_rep(q, 2, y))
 
     @pl.when(y == 0)
     def _():
-        for d in range(1, YS):
-            greet(at_rep(q, x, d))
+        greet(at_rep(q, x, 1))
+        greet(at_rep(q, x, 3))
+
+    @pl.when(y == 1)
+    def _():
+        greet(at_rep(q, x, 2))
 
     x_later, y_later = (x > 0).astype(jnp.int32), (y > 0).astype(jnp.int32)
     wait_for(barrier, has_left.astype(jnp.int32) + both.astype(jnp.int32) + o + x_later + y_later + q)
@@ -234,13 +242,13 @@
         piece = ps.at[lax.rem(x + XS - d, XS)]
         return remote(piece, piece, o_send.at[4, d - 1], o_recv.at[4, d - 1], sibling)
 
-    @pl.when(x > 0)
-    def _():
-        answer(at_rep(q, 0, y))
-
-    @pl.when(y > 0)
-    def _():
-        answer(at_rep(q, x, 0))
+    @pl.when(x > 1)
+    def _():
+        answer(at_rep(q, 3 - x, y))
+
+    @pl.when(y > 1)
+    def _():
+        answer(at_rep(q, x, 3 - y))
 
     @pl.when(q == 1)
     def _():
@@ -272,7 +280,17 @@
                 cols = slice(m * lanes, (m + 1) * lanes)
                 nrm[rows, cols] = (tok[rows, cols].astype(F32) * scale * gain[:, cols]).astype(BF16)
 
-    wait_for(here_sem, (1 - x_later) * (XS - 1) + (1 - y_later) * (YS - 1) + (ZS - 1 - q) + c)
+    x_heard = 2 * (1 - x_later) + (x == 1).astype(jnp.int32)
+    y_heard = 2 * (1 - y_later) + (y == 1).astype(jnp.int32)
+    wait_for(here_sem, x_heard + y_heard + (ZS - 1 - q) + c)
+
+    @pl.when(x == 1)
+    def _():
+        answer(at_rep(q, 0, y))
+
+    @pl.when(y == 1)
+    def _():
+        answer(at_rep(q, x, 0))
 
     @pl.when(x == 0)
     def _():

time: 99.6 us -> 102 us (1.024)
  Pallas kernels: 98.1 us -> 101 us
    pallas_call x1, Pallas kernels: 96.3 us -> 99 us  [local(): pl.pallas_call(kernel, out_shape=tuple((pltpu.VMEM(*result) for result in...]
where the time goes in v6:
time: 102 us
  Pallas kernels  101 us (99%)
  between operations  1.29 us (1%)
    pallas_call x1, Pallas kernels, local(): pl.pallas_call(kernel, out_shape=tuple((pltpu.VMEM(*result) for result in...  99 us

profile of v6, /device:TPU:1, one launch (start us, length us, event | category | flops | bytes accessed | tf_op | source)
XLA Modules:
  0.0 102.1 jit_solution(16366850834845332700)
XLA Ops:
  1.3 99.0 %outer_and_keys.1 = (bf16[384,512]{1,0:T(8,128)(2,1)S(1)}, f32[1024,512]{1,0:T(8,128)S(1)}, f32[4,2,8,128]{3,2,1,0:T(8,128)S(1)}, f32[16,8192]{1,0:T(8,128)S(1)}, f32[16,8192]{1,0:T(8,128)S(1)}) custom-call(bf16[384,8192]{1,0:T(8,128)(2,1)} %tok_hbm.1, bf16[1024,512]{1,0:T(8,128)(2,1)} %bitcast.5, bf16[384,512]{1,0:T(8,128)(2,1)} %kg_hbm.1, ...), custom_call_target="tpu_custom_call" | custom-call | flops 9663676416 | bytes 16777216 | tf_op jit(solution)/shard_map/outer_and_keys/pallas_call | solution.py:627
  100.3 1.8 %write_out.1 = (bf16[384,512]{1,0:T(8,128)(2,1)}, f32[1024,512]{1,0:T(8,128)}, f32[4,2,8,128]{3,2,1,0:T(8,128)}, f32[16,8192]{1,0:T(8,128)}, f32[16,8192]{1,0:T(8,128)}) custom-call(bf16[384,512]{1,0:T(8,128)(2,1)S(1)} %get-tuple-element.15.refs_0_, f32[1024,512]{1,0:T(8,128)S(1)} %get-tuple-element.16.refs_1_, ...), custom_call_target="tpu_custom_call" | custom-call | tf_op jit(solution)/shard_map/write_out/pallas_call | solution.py:678

commit v7 on v5

--- a/solution.py
+++ b/solution.py
@@ -347,23 +347,14 @@
     gain_swap = remote(g_own.at[o], g_sib, g_send.at[0], g_recv.at[0], sibling)
 
     def gain_copy(d):
-        to = lax.rem(z + d, CHIPS)
-        return remote(g_own.at[c, to], g_z.at[z], g_send.at[d], g_recv.at[d], at_chip(to))
+        return remote(g_z.at[z], g_z.at[z], g_send.at[d], g_recv.at[d], at_chip(lax.rem(z + d, CHIPS)))
 
     def gain_wait(d):
         slot = g_z.at[lax.rem(z + CHIPS - d, CHIPS)]
         return remote(slot, slot, g_send.at[d], g_recv.at[d], sibling)
 
-    def gain_out(d):
-        sem = CHIPS + d - 1
-        return remote(g_fin.at[z, c], g_fin.at[z, c], g_send.at[sem], g_recv.at[sem], at_chip(lax.rem(z + d, CHIPS)))
-
-    def gain_in(d):
-        slot, sem = g_fin.at[lax.rem(z + CHIPS - d, CHIPS), c], CHIPS + d - 1
-        return remote(slot, slot, g_send.at[sem], g_recv.at[sem], sibling)
-
-    gain_back = remote(g_fin.at[:, c], g_fin.at[:, c], g_send.at[2 * CHIPS - 1], g_recv.at[2 * CHIPS - 1], sibling)
-    gain_back_in = remote(g_fin.at[:, o], g_fin.at[:, o], g_send.at[2 * CHIPS - 1], g_recv.at[2 * CHIPS - 1], sibling)
+    gain_back = remote(g_fin.at[:, c], g_fin.at[:, c], g_send.at[CHIPS], g_recv.at[CHIPS], sibling)
+    gain_back_in = remote(g_fin.at[:, o], g_fin.at[:, o], g_send.at[CHIPS], g_recv.at[CHIPS], sibling)
 
     @pl.loop(0, STEPS)
     def _(s):
@@ -422,18 +413,14 @@
                     mo[:, cols] = moment
                     op[:, cols] = op[:, cols] - rate * (pseudo + OUTER_MOMENTUM * moment)
 
-        @pl.when(s == LAST + 1)
+        @pl.when(s == STEPS - 1)
         def _():
             for d in range(1, CHIPS):
                 gain_wait(d).wait_recv()
-            g_fin[z, c] = (g_z[0] + g_z[1]) + (g_z[2] + g_z[3])
-            for d in range(1, CHIPS):
-                gain_out(d).start()
-
-        @pl.when(s == STEPS - 1)
-        def _():
-            for d in range(1, CHIPS):
-                gain_in(d).wait_recv()
+            total = (g_z[0].astype(F32) + g_z[1].astype(F32)) + (g_z[2].astype(F32) + g_z[3].astype(F32))
+            size = total.shape[0] // CHIPS
+            for j in range(CHIPS):
+                g_fin[j, c] = total[j * size : (j + 1) * size]
             gain_back.start()
 
         @pl.when(jnp.logical_and(has_right, s > 1))
@@ -465,7 +452,6 @@
         def _():
             for d in range(1, CHIPS):
                 gain_copy(d).wait_send()
-                gain_out(d).wait_send()
 
         @pl.when(k == CHIPS - 1)
         def _():
@@ -534,13 +520,12 @@
         @pl.when(s == LAST - 1)
         def _():
             gain_swap.wait_recv()
-            g_own[c] = g_own[c] + g_sib[...]
+            g_z[z] = (g_own[c] + g_sib[...]).reshape(g_z.shape[1:]).astype(BF16)
             for d in range(1, CHIPS):
                 gain_copy(d).start()
-            g_z[z] = g_own[c, z]
-
-        early, late = s < LAST + 2 - CHUNKS, jnp.logical_and(s >= LAST, s < LAST + 2)
-        n = s + CHUNKS - (CHUNKS - 2) * late.astype(jnp.int32)
+
+        early, late = s < LAST + 2 - CHUNKS, jnp.logical_and(s >= LAST - 1, s <= LAST)
+        n = s + CHUNKS - late.astype(jnp.int32)
         due = jnp.logical_or(early, late)
 
         @pl.when(jnp.logical_and(has_right, due))
@@ -621,7 +606,7 @@
             pltpu.VMEM((rows, kw), F32),
             pltpu.VMEM((CORES, CHIPS, shard // lanes, lanes), F32),
             pltpu.VMEM((CHIPS, shard // lanes, lanes), F32),
-            pltpu.VMEM((CHIPS, shard // lanes, lanes), F32),
+            pltpu.VMEM((CHIPS, width // CORES // lanes, lanes), BF16),
             pltpu.VMEM((XS, frag, xcols), BF16),
             pltpu.VMEM((YS, frag, ycols), F32),
             pltpu.VMEM((YS, frag, ycols), F32),
@@ -639,8 +624,8 @@
             dma((CHIPS, CHUNKS)),
             dma((CHIPS, CHUNKS)),
             dma((CHIPS, CHUNKS)),
-            dma((2 * CHIPS,)),
-            dma((2 * CHIPS,)),
+            dma((CHIPS + 1,)),
+            dma((CHIPS + 1,)),
             dma((5, 3)),
             dma((5, 3)),
             pltpu.SemaphoreType.REGULAR,

time: 99.6 us -> 99.5 us (level)
  no operation moved by 1% of the time
where the time goes in v7:
time: 99.5 us; the launch traced here: 99.4 us
  Pallas kernels  98.1 us (99%)
  between operations  1.29 us (1%)
    pallas_call x1, Pallas kernels, local(): pl.pallas_call(kernel, out_shape=tuple((pltpu.VMEM(*result) for result in...  96.2 us

profile of v7, /device:TPU:1, one launch (start us, length us, event | category | flops | bytes accessed | tf_op | source)
XLA Modules:
  0.0 99.4 jit_solution(6207767455502076070)
XLA Ops:
  1.3 96.2 %outer_and_keys.1 = (bf16[384,512]{1,0:T(8,128)(2,1)S(1)}, f32[1024,512]{1,0:T(8,128)S(1)}, f32[4,2,8,128]{3,2,1,0:T(8,128)S(1)}, f32[16,8192]{1,0:T(8,128)S(1)}, f32[16,8192]{1,0:T(8,128)S(1)}) custom-call(bf16[384,8192]{1,0:T(8,128)(2,1)} %tok_hbm.1, bf16[1024,512]{1,0:T(8,128)(2,1)} %bitcast.5, bf16[384,512]{1,0:T(8,128)(2,1)} %kg_hbm.1, ...), custom_call_target="tpu_custom_call" | custom-call | flops 9663676416 | bytes 16777216 | tf_op jit(solution)/shard_map/outer_and_keys/pallas_call | solution.py:594
  97.5 1.8 %write_out.1 = (bf16[384,512]{1,0:T(8,128)(2,1)}, f32[1024,512]{1,0:T(8,128)}, f32[4,2,8,128]{3,2,1,0:T(8,128)}, f32[16,8192]{1,0:T(8,128)}, f32[16,8192]{1,0:T(8,128)}) custom-call(bf16[384,512]{1,0:T(8,128)(2,1)S(1)} %get-tuple-element.15.refs_0_, f32[1024,512]{1,0:T(8,128)S(1)} %get-tuple-element.16.refs_1_, ...), custom_call_target="tpu_custom_call" | custom-call | tf_op jit(solution)/shard_map/write_out/pallas_call | solution.py:645
